TPU v7x, 256 devices: a whole 4x4x8 slice. The times are simulated.
256 devices in a mesh: grp: 8 (over y, core), box: 32 (over x, z).
Axes of the slice: x: 4, y: 4, z: 8, core: 2. Of those that a mesh axis runs over, the one named last changes fastest.
Arguments:
- source: float32 [128, 256, 256], P('grp', 'box'), may hold values from -16 to 30
- alpha: float32 [128, 256, 256], P('grp', 'box'), may hold values from 0.02 to 0.4
- beta: float32 [128, 256, 256], P('grp', 'box'), may hold values from 0.3 to 3
Outputs:
- correction: float32 [128, 256, 256], P('grp', 'box')
All inputs are finite; a program needn't handle non-finite values.
Results may differ from a plain program's by a relative error of at most 0.00002.
Values sent between devices are 32-bit elements; how exact they have to be, the bound alone decides.
A program may use at most 128 MiB of HBM per device.

v0:
```python
from functools import partial

import jax
import jax.numpy as jnp
from jax import lax
from jax.sharding import PartitionSpec as P

SMOOTH = 4
BOTTOM = 16


SMOOTH_LOW = 0.25
BOTTOM_LOW = 0.02
UPPER_BOUND = 2.0


def padded_2(cells, sides, width):
    for axis, dim in sides:
        count = lax.axis_size(axis)
        ends = count - 1
        head = lax.slice_in_dim(cells, 0, width, axis=dim)
        tail = lax.slice_in_dim(cells, cells.shape[dim] - width, cells.shape[dim], axis=dim)
        cells = jnp.concatenate(
            [
                lax.ppermute(tail, axis, [(i, (i + 1) % count) for i in range(ends)]),
                cells,
                lax.ppermute(head, axis, [((i + 1) % count, i) for i in range(ends)]),
            ],
            axis=dim,
        )
    return cells


def fine_pad(field):
    grown = padded_2(field, (("grp", 0), ("box", 1)), 1)
    return jnp.pad(grown, ((0, 0), (0, 0), (1, 1)))


def middle_pad(field):
    grown = padded_2(field, (("box", 1),), 1)
    return jnp.pad(grown, ((1, 1), (0, 0), (1, 1)))


def coarse_pad(field):
    grown = padded_2(field, (("box", 1),), 1)
    return jnp.pad(grown, ((1, 1), (0, 0), (1, 1)))


def couplings(alpha, beta, scale, padder):
    padded = padder(beta)
    east = scale * 0.5 * (beta + padded[2:, 1:-1, 1:-1])
    west = scale * 0.5 * (beta + padded[:-2, 1:-1, 1:-1])
    north = scale * 0.5 * (beta + padded[1:-1, 2:, 1:-1])
    south = scale * 0.5 * (beta + padded[1:-1, :-2, 1:-1])
    above = scale * 0.5 * (beta + padded[1:-1, 1:-1, 2:])
    below = scale * 0.5 * (beta + padded[1:-1, 1:-1, :-2])
    diagonal = alpha + east + west + north + south + above + below
    return (diagonal, east, west, north, south, above, below)


def operate(field, table, padder):
    padded = padder(field)
    result = (
        table[0] * field - table[1] * padded[2:, 1:-1, 1:-1] - table[2] * padded[:-2, 1:-1, 1:-1]
    )
    result = result - table[3] * padded[1:-1, 2:, 1:-1] - table[4] * padded[1:-1, :-2, 1:-1]
    return result - table[5] * padded[1:-1, 1:-1, 2:] - table[6] * padded[1:-1, 1:-1, :-2]


def restrict(field):
    sizes = field.shape
    return field.reshape(sizes[0] // 2, 2, sizes[1] // 2, 2, sizes[2] // 2, 2).mean(axis=(1, 3, 5))


def prolong(field):
    return jnp.repeat(jnp.repeat(jnp.repeat(field, 2, 0), 2, 1), 2, 2)


def chebyshev(operator, diagonal, source, guess, degree, lower):
    middle = (UPPER_BOUND + lower) / 2.0
    spread = (UPPER_BOUND - lower) / 2.0
    ratio_base = middle / spread
    factor_now = 1.0 / ratio_base
    if guess is None:
        residual = source
        approx = jnp.zeros_like(source)
    else:
        residual = source - operator(guess)
        approx = guess
    update = residual / (diagonal * middle)
    approx = approx + update
    for k in range(degree - 1):
        residual = source - operator(approx)
        factor_next = 1.0 / (2.0 * ratio_base - factor_now)
        update = (
            factor_next * factor_now * update + 2.0 * factor_next / spread * residual / diagonal
        )
        approx = approx + update
        factor_now = factor_next
    return approx


def coarse_solve(source_five, alpha_five, beta_five):
    coarse = couplings(alpha_five, beta_five, 0.0625, coarse_pad)
    coarse_op = partial(operate, table=coarse, padder=coarse_pad)
    return chebyshev(coarse_op, coarse[0], source_five, None, BOTTOM, BOTTOM_LOW)


def shards(source, alpha, beta):
    fine = couplings(alpha, beta, 1.0, fine_pad)
    fine_op = partial(operate, table=fine, padder=fine_pad)
    approx_three = chebyshev(fine_op, fine[0], source, None, SMOOTH, SMOOTH_LOW)
    local_four = restrict(source - fine_op(approx_three))
    source_four, alpha_four, beta_four = (
        lax.all_gather(local_four, "grp", axis=0, tiled=True),
        lax.all_gather(restrict(alpha), "grp", axis=0, tiled=True),
        lax.all_gather(restrict(beta), "grp", axis=0, tiled=True),
    )
    middle_table = couplings(alpha_four, beta_four, 0.25, middle_pad)
    middle_op = partial(operate, table=middle_table, padder=middle_pad)
    approx_four = chebyshev(middle_op, middle_table[0], source_four, None, SMOOTH, SMOOTH_LOW)
    source_five = restrict(source_four - middle_op(approx_four))
    solved = coarse_solve(source_five, restrict(alpha_four), restrict(beta_four))
    approx_four = chebyshev(
        middle_op, middle_table[0], source_four, approx_four + prolong(solved), SMOOTH, SMOOTH_LOW
    )
    own_rows = source.shape[0] // 2
    own_four = lax.dynamic_slice_in_dim(approx_four, lax.axis_index("grp") * own_rows, own_rows, 0)
    return chebyshev(fine_op, fine[0], source, approx_three + prolong(own_four), SMOOTH, SMOOTH_LOW)


def solution(mesh):
    in_specs = (P("grp", "box", None), P("grp", "box", None), P("grp", "box", None))
    out_specs = P("grp", "box", None)
    return jax.shard_map(shards, mesh=mesh, in_specs=in_specs, out_specs=out_specs, check_vma=False)
```

profile of v0, /device:TPU:1, one launch (start us, length us, event | category | flops | bytes accessed | tf_op | source)
XLA Modules:
  0.0 535.9 jit_solution(13377192842649650574)
XLA Ops:
  0.7 4.6 collective-permute-start.1
  10.3 3.5 collective-permute-start.3
  28.4 3.5 collective-permute-start.7
  33.4 10.5 %reshape.38 = f32[8,2,4,2,128,2]{5,4,3,2,1,0:T(8,128)} reshape(f32[16,8,256]{2,1,0:T(8,128)} %param.5) | data formatting | bytes 262144 | tf_op jit(solution)/shard_map/reshape | solution.py:72
  44.0 4.1 reduce_sum.56
  55.8 5.3 collective-permute-start.11
  62.4 12.2 %all_gather.11 = f32[64,4,128]{2,1,0:T(4,128)S(1)} all-gather(f32[8,4,128]{2,1,0:T(4,128)S(1)} %broadcast_multiply_fusion.2), channel_id=1, replica_groups=mesh['grp'=8,'box'=32] {'grp'}, dimensions={0}, use_global_device_ids=true | all-gather | bytes 147456 | tf_op jit(solution)/shard_map/all_gather | solution.py:117
  80.3 5.5 %collective-permute-start.20 = (f32[64,1,128]{0,2,1:T(8,128)S(1)}, f32[64,1,128]{0,2,1:T(8,128)S(1)}, u32[]{:S(2)}, u32[]{:S(2)}) collective-permute-start(f32[64,1,128]{0,2,1:T(8,128)S(1)} %get-tuple-element.77), channel_id=1, source_target_pairs={{0,1},{1,2},{2,3},{3,4},{4,5},{5,6},{6,7},{7,8},{8,9},{9,10},{10,1... | collective-permute-start | bytes 98312 | tf_op jit(solution)/shard_map/ppermute | solution.py:25
  87.1 9.8 %reshape.37 = f32[8,2,4,2,128,2]{5,4,3,2,1,0:T(8,128)} reshape(f32[16,8,256]{2,1,0:T(8,128)S(1)} %copy-done.1) | data formatting | bytes 262144 | tf_op jit(solution)/shard_map/reshape | solution.py:72
  96.9 4.1 reduce_sum.55
  101.0 4.3 collective-permute-start.15
  110.6 5.1 collective-permute-start.17
  117.6 12.7 %all_gather.10 = f32[64,4,128]{2,1,0:T(4,128)S(1)} all-gather(f32[8,4,128]{2,1,0:T(4,128)S(1)} %broadcast_multiply_fusion.3), channel_id=1, replica_groups=mesh['grp'=8,'box'=32] {'grp'}, dimensions={0}, use_global_device_ids=true | all-gather | bytes 147456 | tf_op jit(solution)/shard_map/all_gather | solution.py:116
  130.6 4.1 collective-permute-start.19
  136.2 4.5 collective-permute-done.18
  141.1 9.8 %reshape.36 = f32[8,2,4,2,128,2]{5,4,3,2,1,0:T(8,128)} reshape(f32[16,8,256]{2,1,0:T(8,128)S(1)} %fusion.159) | data formatting | bytes 262144 | tf_op jit(solution)/shard_map/reshape | solution.py:72
  150.9 4.1 reduce_sum.54
  155.0 14.1 %all_gather.9 = f32[64,4,128]{2,1,0:T(4,128)S(1)} all-gather(f32[8,4,128]{2,1,0:T(4,128)S(1)} %broadcast_multiply_fusion.4), channel_id=1, replica_groups=mesh['grp'=8,'box'=32] {'grp'}, dimensions={0}, use_global_device_ids=true | all-gather | bytes 147456 | tf_op jit(solution)/shard_map/all_gather | solution.py:115
  170.3 4.9 collective-permute-start.22
  176.5 9.8 %reshape.41 = f32[32,2,2,2,64,2]{5,4,1,0,3,2:T(8,128)} reshape(f32[64,4,128]{2,0,1:T(8,128)S(1)} %copy.522) | data formatting | bytes 262144 | tf_op jit(solution)/shard_map/reshape | solution.py:72
  186.2 4.0 reduce_sum.59
  191.2 4.3 collective-permute-start.24
  196.8 3.6 collective-permute-done.25
  203.8 4.0 collective-permute-start.26
  209.7 4.0 collective-permute-start.30
  215.6 10.5 %reshape.40 = f32[32,2,2,2,64,2]{5,4,1,0,3,2:T(8,128)} reshape(f32[64,4,128]{2,0,1:T(8,128)} %copy.521) | data formatting | bytes 262144 | tf_op jit(solution)/shard_map/reshape | solution.py:72
  226.2 4.1 reduce_sum.58
  234.0 4.9 collective-permute-start.28
  244.9 9.8 %reshape.39 = f32[32,2,2,2,64,2]{5,4,1,0,3,2:T(8,128)} reshape(f32[64,4,128]{2,0,1:T(8,128)S(1)} %copy.520) | data formatting | bytes 262144 | tf_op jit(solution)/shard_map/reshape | solution.py:72
  254.7 4.1 reduce_sum.57
  259.6 4.0 collective-permute-start.32
  265.0 4.4 collective-permute-done.33
  269.6 4.6 collective-permute-start.34
  279.2 4.0 collective-permute-start.36
  284.4 4.4 collective-permute-done.37
  289.1 5.8 %collective-permute-start.38 = (f32[32,1,64]{2,0,1:T(8,128)S(1)}, f32[32,1,64]{2,0,1:T(8,128)S(1)}, u32[]{:S(2)}, u32[]{:S(2)}) collective-permute-start(f32[32,1,64]{2,0,1:T(8,128)S(1)} %get-tuple-element.137), channel_id=1, source_target_pairs={{0,1},{1,2},{2,3},{3,4},{4,5},{5,6},{6,7},{7,8},{8,9},{9,10},{10,1... | collective-permute-start | bytes 24584 | tf_op jit(solution)/shard_map/ppermute | solution.py:25
  299.6 4.3 collective-permute-start.40
  308.6 4.2 collective-permute-start.42
  317.6 3.9 collective-permute-start.44
  326.3 3.8 collective-permute-start.46
  334.8 4.0 collective-permute-start.48
  343.6 4.0 collective-permute-start.50
  352.3 4.3 collective-permute-start.52
  361.4 3.7 collective-permute-start.54
  369.8 4.3 collective-permute-start.56
  378.9 3.7 collective-permute-start.58
  387.3 4.0 collective-permute-start.60
  396.3 4.0 collective-permute-start.62
  401.7 3.7 collective-permute-done.63
  406.2 4.5 collective-permute-start.64
  412.0 3.7 collective-permute-done.65
  416.5 4.0 collective-permute-start.66
  421.8 3.7 collective-permute-done.67
  427.3 3.7 collective-permute-start.68
  432.3 3.7 collective-permute-done.69
  439.3 30.2 %collective-permute-start.71 = (f32[1,8,256]{2,1,0:T(8,128)S(1)}, f32[1,8,256]{2,1,0:T(8,128)S(1)}, u32[]{:S(2)}, u32[]{:S(2)}) collective-permute-start(f32[1,8,256]{2,1,0:T(8,128)S(1)} %get-tuple-element.103), channel_id=1, source_target_pairs={{0,32},{32,64},{64,96},{96,128},{128,160},{160,192},{192,224},{1,3... | collective-permute-start | bytes 24584 | tf_op jit(solution)/shard_map/ppermute | solution.py:25
  474.6 3.7 collective-permute-start.73
  479.7 3.5 collective-permute-done.72
  491.8 3.7 collective-permute-start.77
  496.8 3.5 collective-permute-done.76
  509.0 3.7 collective-permute-start.81
  514.0 3.5 collective-permute-done.80
  526.2 3.7 collective-permute-start.85
  531.2 3.5 collective-permute-done.84
  (295 shorter events, 182.5 us)
Async XLA Ops:
  0.7 6.5 %collective-permute-start.1 = (f32[1,8,256]{2,1,0:T(8,128)S(1)}, f32[1,8,256]{2,1,0:T(8,128)S(1)}, u32[]{:S(2)}, u32[]{:S(2)}) collective-permute-start(f32[1,8,256]{2,1,0:T(8,128)S(1)} %get-tuple-element.113), channel_id=1, source_target_pairs={{0,32},{32,64},{64,96},{96,128},{128,160},{160,192},{192,224},{1,3... | collective-permute-start | bytes 24584 | tf_op jit(solution)/shard_map/ppermute | solution.py:25
  5.3 5.0 collective-permute-start
  20.2 5.1 collective-permute-start.5
  23.4 5.0 collective-permute-start.4
  28.4 19.6 %collective-permute-start.7 = (f32[18,1,256]{2,1,0:T(1,128)S(1)}, f32[18,1,256]{2,1,0:T(1,128)S(1)}, u32[]{:S(2)}, u32[]{:S(2)}) collective-permute-start(f32[18,1,256]{2,1,0:T(1,128)S(1)} %get-tuple-element.93), channel_id=1, source_target_pairs={{0,1},{1,2},{2,3},{3,4},{4,5},{5,6},{6,7},{7,8},{8,9},{9,10},{10,1... | collective-permute-start | bytes 55304 | tf_op jit(solution)/shard_map/ppermute | solution.py:25
  32.0 16.0 %collective-permute-start.6 = (f32[18,1,256]{2,1,0:T(1,128)S(1)}, f32[18,1,256]{2,1,0:T(1,128)S(1)}, u32[]{:S(2)}, u32[]{:S(2)}) collective-permute-start(f32[18,1,256]{2,1,0:T(1,128)S(1)} %get-tuple-element.94), channel_id=1, source_target_pairs={{1,0},{2,1},{3,2},{4,3},{5,4},{6,5},{7,6},{8,7},{9,8},{10,9},{11,1... | collective-permute-start | bytes 55304 | tf_op jit(solution)/shard_map/ppermute | solution.py:27
  50.9 5.0 collective-permute-start.8
  55.8 19.0 %collective-permute-start.11 = (f32[18,1,256]{2,1,0:T(1,128)S(1)}, f32[18,1,256]{2,1,0:T(1,128)S(1)}, u32[]{:S(2)}, u32[]{:S(2)}) collective-permute-start(f32[18,1,256]{2,1,0:T(1,128)S(1)} %get-tuple-element.91), channel_id=1, source_target_pairs={{0,1},{1,2},{2,3},{3,4},{4,5},{5,6},{6,7},{7,8},{8,9},{9,10},{10,1... | collective-permute-start | bytes 55304 | tf_op jit(solution)/shard_map/ppermute | solution.py:25
  61.1 13.7 %collective-permute-start.10 = (f32[18,1,256]{2,1,0:T(1,128)S(1)}, f32[18,1,256]{2,1,0:T(1,128)S(1)}, u32[]{:S(2)}, u32[]{:S(2)}) collective-permute-start(f32[18,1,256]{2,1,0:T(1,128)S(1)} %get-tuple-element.92), channel_id=1, source_target_pairs={{1,0},{2,1},{3,2},{4,3},{5,4},{6,5},{7,6},{8,7},{9,8},{10,9},{11,1... | collective-permute-start | bytes 55304 | tf_op jit(solution)/shard_map/ppermute | solution.py:27
  75.4 25.6 %collective-permute-start.13 = (f32[1,8,256]{2,1,0:T(8,128)S(1)}, f32[1,8,256]{2,1,0:T(8,128)S(1)}, u32[]{:S(2)}, u32[]{:S(2)}) collective-permute-start(f32[1,8,256]{2,1,0:T(8,128)S(1)} %get-tuple-element.107), channel_id=1, source_target_pairs={{0,32},{32,64},{64,96},{96,128},{128,160},{160,192},{192,224},{1,3... | collective-permute-start | bytes 24584 | tf_op jit(solution)/shard_map/ppermute | solution.py:25
  78.4 22.6 %collective-permute-start.12 = (f32[1,8,256]{2,1,0:T(8,128)S(1)}, f32[1,8,256]{2,1,0:T(8,128)S(1)}, u32[]{:S(2)}, u32[]{:S(2)}) collective-permute-start(f32[1,8,256]{2,1,0:T(8,128)S(1)} %get-tuple-element.108), channel_id=1, source_target_pairs={{32,0},{64,32},{96,64},{128,96},{160,128},{192,160},{224,192},{33,... | collective-permute-start | bytes 24584 | tf_op jit(solution)/shard_map/ppermute | solution.py:27
  80.3 55.6 %collective-permute-start.20 = (f32[64,1,128]{0,2,1:T(8,128)S(1)}, f32[64,1,128]{0,2,1:T(8,128)S(1)}, u32[]{:S(2)}, u32[]{:S(2)}) collective-permute-start(f32[64,1,128]{0,2,1:T(8,128)S(1)} %get-tuple-element.77), channel_id=1, source_target_pairs={{0,1},{1,2},{2,3},{3,4},{4,5},{5,6},{6,7},{7,8},{8,9},{9,10},{10,1... | collective-permute-start | bytes 98312 | tf_op jit(solution)/shard_map/ppermute | solution.py:25
  85.8 50.1 %collective-permute-start.21 = (f32[64,1,128]{0,2,1:T(8,128)S(1)}, f32[64,1,128]{0,2,1:T(8,128)S(1)}, u32[]{:S(2)}, u32[]{:S(2)}) collective-permute-start(f32[64,1,128]{0,2,1:T(8,128)S(1)} %get-tuple-element.78), channel_id=1, source_target_pairs={{1,0},{2,1},{3,2},{4,3},{5,4},{6,5},{7,6},{8,7},{9,8},{10,9},{11,1... | collective-permute-start | bytes 98312 | tf_op jit(solution)/shard_map/ppermute | solution.py:27
  101.0 5.6 %collective-permute-start.15 = (f32[18,1,256]{2,1,0:T(1,128)S(1)}, f32[18,1,256]{2,1,0:T(1,128)S(1)}, u32[]{:S(2)}, u32[]{:S(2)}) collective-permute-start(f32[18,1,256]{2,1,0:T(1,128)S(1)} %get-tuple-element.89), channel_id=1, source_target_pairs={{0,1},{1,2},{2,3},{3,4},{4,5},{5,6},{6,7},{7,8},{8,9},{9,10},{10,1... | collective-permute-start | bytes 55304 | tf_op jit(solution)/shard_map/ppermute | solution.py:25
  110.6 19.9 %collective-permute-start.17 = (f32[1,8,256]{2,1,0:T(8,128)S(1)}, f32[1,8,256]{2,1,0:T(8,128)S(1)}, u32[]{:S(2)}, u32[]{:S(2)}) collective-permute-start(f32[1,8,256]{2,1,0:T(8,128)S(1)} %get-tuple-element.105), channel_id=1, source_target_pairs={{0,32},{32,64},{64,96},{96,128},{128,160},{160,192},{192,224},{1,3... | collective-permute-start | bytes 24584 | tf_op jit(solution)/shard_map/ppermute | solution.py:25
  115.7 14.8 %collective-permute-start.16 = (f32[1,8,256]{2,1,0:T(8,128)S(1)}, f32[1,8,256]{2,1,0:T(8,128)S(1)}, u32[]{:S(2)}, u32[]{:S(2)}) collective-permute-start(f32[1,8,256]{2,1,0:T(8,128)S(1)} %get-tuple-element.106), channel_id=1, source_target_pairs={{32,0},{64,32},{96,64},{128,96},{160,128},{192,160},{224,192},{33,... | collective-permute-start | bytes 24584 | tf_op jit(solution)/shard_map/ppermute | solution.py:27
  130.6 5.6 %collective-permute-start.19 = (f32[18,1,256]{2,1,0:T(1,128)S(1)}, f32[18,1,256]{2,1,0:T(1,128)S(1)}, u32[]{:S(2)}, u32[]{:S(2)}) collective-permute-start(f32[18,1,256]{2,1,0:T(1,128)S(1)} %get-tuple-element.87), channel_id=1, source_target_pairs={{0,1},{1,2},{2,3},{3,4},{4,5},{5,6},{6,7},{7,8},{8,9},{9,10},{10,1... | collective-permute-start | bytes 55304 | tf_op jit(solution)/shard_map/ppermute | solution.py:25
  134.6 6.0 %collective-permute-start.18 = (f32[18,1,256]{2,1,0:T(1,128)S(1)}, f32[18,1,256]{2,1,0:T(1,128)S(1)}, u32[]{:S(2)}, u32[]{:S(2)}) collective-permute-start(f32[18,1,256]{2,1,0:T(1,128)S(1)} %get-tuple-element.88), channel_id=1, source_target_pairs={{1,0},{2,1},{3,2},{4,3},{5,4},{6,5},{7,6},{8,7},{9,8},{10,9},{11,1... | collective-permute-start | bytes 55304 | tf_op jit(solution)/shard_map/ppermute | solution.py:27
  170.3 20.0 %collective-permute-start.22 = (f32[64,1,128]{0,2,1:T(8,128)S(1)}, f32[64,1,128]{0,2,1:T(8,128)S(1)}, u32[]{:S(2)}, u32[]{:S(2)}) collective-permute-start(f32[64,1,128]{0,2,1:T(8,128)S(1)} %get-tuple-element.75), channel_id=1, source_target_pairs={{0,1},{1,2},{2,3},{3,4},{4,5},{5,6},{6,7},{7,8},{8,9},{9,10},{10,1... | collective-permute-start | bytes 98312 | tf_op jit(solution)/shard_map/ppermute | solution.py:25
  175.1 15.2 %collective-permute-start.23 = (f32[64,1,128]{0,2,1:T(8,128)S(1)}, f32[64,1,128]{0,2,1:T(8,128)S(1)}, u32[]{:S(2)}, u32[]{:S(2)}) collective-permute-start(f32[64,1,128]{0,2,1:T(8,128)S(1)} %get-tuple-element.76), channel_id=1, source_target_pairs={{1,0},{2,1},{3,2},{4,3},{5,4},{6,5},{7,6},{8,7},{9,8},{10,9},{11,1... | collective-permute-start | bytes 98312 | tf_op jit(solution)/shard_map/ppermute | solution.py:27
  191.2 5.6 %collective-permute-start.24 = (f32[64,1,128]{0,2,1:T(8,128)S(1)}, f32[64,1,128]{0,2,1:T(8,128)S(1)}, u32[]{:S(2)}, u32[]{:S(2)}) collective-permute-start(f32[64,1,128]{0,2,1:T(8,128)S(1)} %get-tuple-element.73), channel_id=1, source_target_pairs={{0,1},{1,2},{2,3},{3,4},{4,5},{5,6},{6,7},{7,8},{8,9},{9,10},{10,1... | collective-permute-start | bytes 98312 | tf_op jit(solution)/shard_map/ppermute | solution.py:25
  195.5 5.0 collective-permute-start.25
  203.8 26.4 %collective-permute-start.26 = (f32[64,1,128]{0,2,1:T(8,128)}, f32[64,1,128]{0,2,1:T(8,128)}, u32[]{:S(2)}, u32[]{:S(2)}) collective-permute-start(f32[64,1,128]{0,2,1:T(8,128)} %get-tuple-element.71), channel_id=1, source_target_pairs={{0,1},{1,2},{2,3},{3,4},{4,5},{5,6},{6,7},{7,8},{8,9},{9,10},{10,1... | collective-permute-start | bytes 98312 | tf_op jit(solution)/shard_map/ppermute | solution.py:25
  207.8 22.5 %collective-permute-start.27 = (f32[64,1,128]{0,2,1:T(8,128)}, f32[64,1,128]{0,2,1:T(8,128)}, u32[]{:S(2)}, u32[]{:S(2)}) collective-permute-start(f32[64,1,128]{0,2,1:T(8,128)} %get-tuple-element.72), channel_id=1, source_target_pairs={{1,0},{2,1},{3,2},{4,3},{5,4},{6,5},{7,6},{8,7},{9,8},{10,9},{11,1... | collective-permute-start | bytes 98312 | tf_op jit(solution)/shard_map/ppermute | solution.py:27
  209.7 30.5 %collective-permute-start.30 = (f32[32,1,64]{2,0,1:T(8,128)}, f32[32,1,64]{2,0,1:T(8,128)S(1)}, u32[]{:S(2)}, u32[]{:S(2)}) collective-permute-start(f32[32,1,64]{2,0,1:T(8,128)} %get-tuple-element.145), channel_id=1, source_target_pairs={{0,1},{1,2},{2,3},{3,4},{4,5},{5,6},{6,7},{7,8},{8,9},{9,10},{10,1... | collective-permute-start | bytes 24584 | tf_op jit(solution)/shard_map/ppermute | solution.py:25
  213.7 26.6 %collective-permute-start.31 = (f32[32,1,64]{2,0,1:T(8,128)}, f32[32,1,64]{2,0,1:T(8,128)}, u32[]{:S(2)}, u32[]{:S(2)}) collective-permute-start(f32[32,1,64]{2,0,1:T(8,128)} %get-tuple-element.146), channel_id=1, source_target_pairs={{1,0},{2,1},{3,2},{4,3},{5,4},{6,5},{7,6},{8,7},{9,8},{10,9},{11,1... | collective-permute-start | bytes 24584 | tf_op jit(solution)/shard_map/ppermute | solution.py:27
  234.0 7.2 %collective-permute-start.28 = (f32[64,1,128]{0,2,1:T(8,128)S(1)}, f32[64,1,128]{0,2,1:T(8,128)S(1)}, u32[]{:S(2)}, u32[]{:S(2)}) collective-permute-start(f32[64,1,128]{0,2,1:T(8,128)S(1)} %get-tuple-element.69), channel_id=1, source_target_pairs={{0,1},{1,2},{2,3},{3,4},{4,5},{5,6},{6,7},{7,8},{8,9},{9,10},{10,1... | collective-permute-start | bytes 98312 | tf_op jit(solution)/shard_map/ppermute | solution.py:25
  238.9 5.0 collective-permute-start.29
  259.6 5.3 collective-permute-start.32
  263.7 5.7 %collective-permute-start.33 = (f32[32,1,64]{2,0,1:T(8,128)S(1)}, f32[32,1,64]{2,0,1:T(8,128)S(1)}, u32[]{:S(2)}, u32[]{:S(2)}) collective-permute-start(f32[32,1,64]{2,0,1:T(8,128)S(1)} %get-tuple-element.144), channel_id=1, source_target_pairs={{1,0},{2,1},{3,2},{4,3},{5,4},{6,5},{7,6},{8,7},{9,8},{10,9},{11,1... | collective-permute-start | bytes 24584 | tf_op jit(solution)/shard_map/ppermute | solution.py:27
  269.6 6.1 %collective-permute-start.34 = (f32[32,1,64]{2,0,1:T(8,128)S(1)}, f32[32,1,64]{2,0,1:T(8,128)S(1)}, u32[]{:S(2)}, u32[]{:S(2)}) collective-permute-start(f32[32,1,64]{2,0,1:T(8,128)S(1)} %get-tuple-element.141), channel_id=1, source_target_pairs={{0,1},{1,2},{2,3},{3,4},{4,5},{5,6},{6,7},{7,8},{8,9},{9,10},{10,1... | collective-permute-start | bytes 24584 | tf_op jit(solution)/shard_map/ppermute | solution.py:25
  279.2 5.3 collective-permute-start.36
  283.1 5.8 %collective-permute-start.37 = (f32[32,1,64]{2,0,1:T(8,128)S(1)}, f32[32,1,64]{2,0,1:T(8,128)S(1)}, u32[]{:S(2)}, u32[]{:S(2)}) collective-permute-start(f32[32,1,64]{2,0,1:T(8,128)S(1)} %get-tuple-element.140), channel_id=1, source_target_pairs={{1,0},{2,1},{3,2},{4,3},{5,4},{6,5},{7,6},{8,7},{9,8},{10,9},{11,1... | collective-permute-start | bytes 24584 | tf_op jit(solution)/shard_map/ppermute | solution.py:27
  289.1 7.1 %collective-permute-start.38 = (f32[32,1,64]{2,0,1:T(8,128)S(1)}, f32[32,1,64]{2,0,1:T(8,128)S(1)}, u32[]{:S(2)}, u32[]{:S(2)}) collective-permute-start(f32[32,1,64]{2,0,1:T(8,128)S(1)} %get-tuple-element.137), channel_id=1, source_target_pairs={{0,1},{1,2},{2,3},{3,4},{4,5},{5,6},{6,7},{7,8},{8,9},{9,10},{10,1... | collective-permute-start | bytes 24584 | tf_op jit(solution)/shard_map/ppermute | solution.py:25
  299.6 5.6 %collective-permute-start.40 = (f32[32,1,64]{2,0,1:T(8,128)S(1)}, f32[32,1,64]{2,0,1:T(8,128)S(1)}, u32[]{:S(2)}, u32[]{:S(2)}) collective-permute-start(f32[32,1,64]{2,0,1:T(8,128)S(1)} %get-tuple-element.135), channel_id=1, source_target_pairs={{0,1},{1,2},{2,3},{3,4},{4,5},{5,6},{6,7},{7,8},{8,9},{9,10},{10,1... | collective-permute-start | bytes 24584 | tf_op jit(solution)/shard_map/ppermute | solution.py:25
  308.6 5.6 %collective-permute-start.42 = (f32[32,1,64]{2,0,1:T(8,128)S(1)}, f32[32,1,64]{2,0,1:T(8,128)S(1)}, u32[]{:S(2)}, u32[]{:S(2)}) collective-permute-start(f32[32,1,64]{2,0,1:T(8,128)S(1)} %get-tuple-element.133), channel_id=1, source_target_pairs={{0,1},{1,2},{2,3},{3,4},{4,5},{5,6},{6,7},{7,8},{8,9},{9,10},{10,1... | collective-permute-start | bytes 24584 | tf_op jit(solution)/shard_map/ppermute | solution.py:25
  317.6 5.2 collective-permute-start.44
  326.3 5.1 collective-permute-start.46
  334.8 5.3 collective-permute-start.48
  343.6 5.3 collective-permute-start.50
  352.3 5.6 %collective-permute-start.52 = (f32[32,1,64]{2,0,1:T(8,128)S(1)}, f32[32,1,64]{2,0,1:T(8,128)S(1)}, u32[]{:S(2)}, u32[]{:S(2)}) collective-permute-start(f32[32,1,64]{2,0,1:T(8,128)S(1)} %get-tuple-element.123), channel_id=1, source_target_pairs={{0,1},{1,2},{2,3},{3,4},{4,5},{5,6},{6,7},{7,8},{8,9},{9,10},{10,1... | collective-permute-start | bytes 24584 | tf_op jit(solution)/shard_map/ppermute | solution.py:25
  361.4 5.0 collective-permute-start.54
  369.8 5.6 %collective-permute-start.56 = (f32[32,1,64]{2,0,1:T(8,128)S(1)}, f32[32,1,64]{2,0,1:T(8,128)S(1)}, u32[]{:S(2)}, u32[]{:S(2)}) collective-permute-start(f32[32,1,64]{2,0,1:T(8,128)S(1)} %get-tuple-element.119), channel_id=1, source_target_pairs={{0,1},{1,2},{2,3},{3,4},{4,5},{5,6},{6,7},{7,8},{8,9},{9,10},{10,1... | collective-permute-start | bytes 24584 | tf_op jit(solution)/shard_map/ppermute | solution.py:25
  378.9 5.0 collective-permute-start.58
  387.3 5.3 collective-permute-start.60
  396.3 5.3 collective-permute-start.62
  400.4 5.0 collective-permute-start.63
  406.2 5.8 %collective-permute-start.64 = (f32[64,1,128]{0,2,1:T(8,128)S(1)}, f32[64,1,128]{0,2,1:T(8,128)S(1)}, u32[]{:S(2)}, u32[]{:S(2)}) collective-permute-start(f32[64,1,128]{0,2,1:T(8,128)S(1)} %get-tuple-element.65), channel_id=1, source_target_pairs={{0,1},{1,2},{2,3},{3,4},{4,5},{5,6},{6,7},{7,8},{8,9},{9,10},{10,1... | collective-permute-start | bytes 98312 | tf_op jit(solution)/shard_map/ppermute | solution.py:25
  410.6 5.0 collective-permute-start.65
  416.5 5.3 collective-permute-start.66
  420.5 5.0 collective-permute-start.67
  427.3 5.0 collective-permute-start.68
  430.9 5.0 collective-permute-start.69
  439.3 32.2 %collective-permute-start.71 = (f32[1,8,256]{2,1,0:T(8,128)S(1)}, f32[1,8,256]{2,1,0:T(8,128)S(1)}, u32[]{:S(2)}, u32[]{:S(2)}) collective-permute-start(f32[1,8,256]{2,1,0:T(8,128)S(1)} %get-tuple-element.103), channel_id=1, source_target_pairs={{0,32},{32,64},{64,96},{96,128},{128,160},{160,192},{192,224},{1,3... | collective-permute-start | bytes 24584 | tf_op jit(solution)/shard_map/ppermute | solution.py:25
  469.6 5.0 collective-permute-start.70
  474.6 5.1 collective-permute-start.73
  483.7 5.0 collective-permute-start.75
  486.8 5.0 collective-permute-start.74
  491.8 5.1 collective-permute-start.77
  500.9 5.0 collective-permute-start.79
  504.0 5.0 collective-permute-start.78
  509.0 5.1 collective-permute-start.81
  518.1 5.0 collective-permute-start.83
  526.2 5.1 collective-permute-start.85
  (39 other events, 434.2 us)
where the time goes:
time: 542 us; the launch traced here: 536 us
  starting transfers between devices  261 us (48%)
  waiting for transfers between devices  117 us (22%)
  local copies, waits for them, and re-layouts  66.4 us (12%)
  other arithmetic  50 us (9%)
  blocking collectives  39.1 us (7%)
    ppermute x43, starting transfers between devices, padded_2(): lax.ppermute(tail, axis, [(i, (i + 1) % count) for i in range(ends)])  200 us
    ppermute x43, waiting for transfers between devices, padded_2(): lax.ppermute(head, axis, [((i + 1) % count, i) for i in range(ends)])  117 us
    ppermute x43, starting transfers between devices, padded_2(): lax.ppermute(head, axis, [((i + 1) % count, i) for i in range(ends)])  61.7 us
    reshape x6, local copies, waits for them, and re-layouts, restrict(): field.reshape(sizes[0] // 2, 2, sizes[1] // 2, 2, sizes[2] // 2, 2)  60.2 us
    reduce_sum x6, other arithmetic, restrict(): field.reshape(sizes[0] // 2, 2, sizes[1] // 2, 2, sizes[2] // 2, 2)  24.4 us
    all_gather x1, blocking collectives, shards(): lax.all_gather(local_four, 'grp', axis=0, tiled=True)  14.1 us
    add x29, other arithmetic, chebyshev(): approx = approx + update  13 us
    all_gather x1, blocking collectives, shards(): lax.all_gather(restrict(alpha), 'grp', axis=0, tiled=True)  12.7 us
  transfers between devices with their start and end apart: 86, of which 35 were waited for; matrix products, arithmetic and copies ran while one was open for 12% of the time, Pallas kernels for 0%

commit v1 on v0

v1 whole, which is shorter than its diff:
```python
import jax
import jax.numpy as jnp
from jax import lax
from jax.experimental import pallas as pl
from jax.experimental.pallas import tpu as pltpu
from jax.sharding import PartitionSpec as P

SMOOTH = 4
BOTTOM = 16
SMOOTH_LOW = 0.25
BOTTOM_LOW = 0.02
UPPER_BOUND = 2.0

MESH = pl.DeviceIdType.MESH
F32 = jnp.float32
NG, NB = 8, 32
N0, N1, N2 = 16, 8, 256
REACH = 9
MID = REACH + 1
SPAN = 2 * MID + 1

FACES = [(dg, db) for db in (-1, 1, 0) for dg in (0, -1, 1) if (dg, db) != (0, 0)]
WIDE = [(dg, db) for db in (-2, 2, -1, 1, 0) for dg in (0, -1, 1) if (dg, db) != (0, 0)]


def coefficients(degree, lower):
    middle = (UPPER_BOUND + lower) / 2.0
    spread = (UPPER_BOUND - lower) / 2.0
    base = middle / spread
    now = 1.0 / base
    pairs = []
    for _ in range(degree - 1):
        after = 1.0 / (2.0 * base - now)
        pairs.append((after * now, 2.0 * after / spread))
        now = after
    return middle, pairs


def part(step, size, width, origin):
    if step == 0:
        return 0, origin, size
    if step == 2:
        return size - (width - size), origin - width, width - size
    if step == -2:
        return 0, origin + 2 * size, width - size
    width = min(width, size)
    if step == 1:
        return size - width, origin - width, width
    return 0, origin + size, width


def kernel(
    source, alpha, beta, out,
    f3, a3, b3, t3, d3, fd3, x3a, x3b, h3,
    ab4, f4, p4, t4, inv4, d4, fd4, x4a, x4b, w4,
    z5, g5ab, g5f, t5, inv5, fd5, x5a, x5b, q4, w3, u4,
    own_sem, ends,
    s_p1, r_p1, s_ab4, r_ab4, s_f4, r_f4, s_x3, r_x3, s_p4, r_p4,
    s_aba, r_aba, s_abb, r_abb, s_abc, r_abc, s_fa, r_fa, s_fb, r_fb, s_fc, r_fc,
):
    g, b = lax.axis_index("grp"), lax.axis_index("box")
    core, chip = lax.rem(g, 2), g // 2
    sub = 4 * core + chip

    def device(dg, db):
        return (lax.rem(g + dg + NG, NG), lax.rem(b + db + NB, NB))

    def remote(src, dst, send, recv, target):
        copy = pltpu.make_async_remote_copy(
            src_ref=src, dst_ref=dst, send_sem=send, recv_sem=recv, device_id=target, device_id_type=MESH
        )
        copy.start()
        return copy

    started = []

    own = [
        pltpu.make_async_copy(beta, b3.at[pl.ds(5, N0), pl.ds(8, N1), :], own_sem.at[0]),
        pltpu.make_async_copy(alpha, a3.at[pl.ds(4, N0), pl.ds(4, N1), :], own_sem.at[1]),
        pltpu.make_async_copy(source, f3.at[pl.ds(4, N0), pl.ds(4, N1), :], own_sem.at[2]),
    ]
    for copy in own:
        copy.start()

    f4[...] = jnp.zeros_like(f4)

    partners = set(FACES) | set(WIDE) | {(2, 0), (4, 0), (6, 0)}
    partners |= {(0, k) for k in range(-MID, MID + 1) if k}
    partners = sorted(partners, key=lambda p: -abs(p[1]))
    barrier = pltpu.get_barrier_semaphore()
    for dg, db in partners:
        pl.semaphore_signal(barrier, inc=1, device_id=device(dg, db), device_id_type=MESH)

    x3a[...] = jnp.zeros_like(x3a)
    x4a[...] = jnp.zeros_like(x4a)
    x5a[...] = jnp.zeros_like(x5a)
    x5b[...] = jnp.zeros_like(x5b)

    pl.semaphore_wait(barrier, len(partners))

    def halo(src, dst, dg, db, w0, w1, o0, o1, size, send, recv):
        s0, t0, l0 = part(dg, size[0], w0, o0)
        s1, t1, l1 = part(db, size[1], w1, o1)
        return remote(
            src(s0, l0, s1, l1), dst(t0, l0, t1, l1), send, recv, device(dg, db)
        )

    def window(ref):
        return lambda i, n, j, m: ref.at[pl.ds(i, n), pl.ds(j, m), :]

    def window2(ref):
        return lambda i, n, j, m: ref.at[:, pl.ds(i, n), pl.ds(j, m), :]

    def inner(ref, o0, o1):
        return lambda i, n, j, m: ref.at[pl.ds(o0 + i, n), pl.ds(o1 + j, m), :]

    def inner2(ref, o0, o1):
        return lambda i, n, j, m: ref.at[:, pl.ds(o0 + i, n), pl.ds(o1 + j, m), :]

    p1 = []
    for n, (src, dst, w, o0, o1) in enumerate(
        ((beta, b3, 5, 5, 8), (alpha, a3, 4, 4, 4), (source, f3, 4, 4, 4))
    ):
        for k, (dg, db) in enumerate(FACES):
            p1.append(
                halo(window(src), window(dst), dg, db, w, w, o0, o1, (N0, N1), s_p1.at[n, k], r_p1.at[n, k])
            )
    started += p1

    rows256 = lax.broadcasted_iota(jnp.int32, (256, 128), 0)
    cols128 = lax.broadcasted_iota(jnp.int32, (256, 128), 1)
    gather = jnp.where(lax.shift_right_logical(rows256, 1) == cols128, 1.0, 0.0).astype(F32)
    rows128 = lax.broadcasted_iota(jnp.int32, (128, 256), 0)
    cols256 = lax.broadcasted_iota(jnp.int32, (128, 256), 1)
    spread = jnp.where(lax.shift_right_logical(cols256, 1) == rows128, 1.0, 0.0).astype(F32)

    def dot(x, matrix):
        return jnp.dot(x, matrix, precision=lax.Precision.HIGHEST, preferred_element_type=F32)

    def halve(pairs, o1):
        n = pairs.shape[1]
        w4[:, 0:n, :] = dot(pairs.reshape(8 * n, 256), gather).reshape(8, n, 128)
        return 0.125 * (w4[:, pl.ds(o1, 4, stride=2), :] + w4[:, pl.ds(o1 + 1, 4, stride=2), :])

    def pack(get, row):
        for i in range(4):
            t = get(2 * i) + get(2 * i + 1)
            z5[pl.ds(row + i, 1), 0:128] = t[0:1] + t[1:2]
            z5[pl.ds(row + i, 1), 128:256] = t[2:3] + t[3:4]

    for copy in own[:2]:
        copy.wait()
    ab4[0, 6:14, 6:10, :] = halve(
        jnp.stack([a3[4 + 2 * i, 4:12, :] + a3[5 + 2 * i, 4:12, :] for i in range(8)]), 0
    )
    ab4[1, 6:14, 6:10, :] = halve(
        jnp.stack([b3[5 + 2 * i, 8:16, :] + b3[6 + 2 * i, 8:16, :] for i in range(8)]), 0
    )
    ab4_copies = []
    for k, (dg, db) in enumerate(WIDE):
        ab4_copies.append(
            halo(inner2(ab4, 6, 6), window2(ab4), dg, db, 6, 6, 6, 6, (8, 4), s_ab4.at[k], r_ab4.at[k])
        )
    started += ab4_copies
    for n in range(2):
        pack(lambda r, n=n: ab4[n, 6 + r, 6:10, :], 4 * n)
    packed = 0.125 * dot(z5[...], gather)
    for n in range(2):
        for i in range(4):
            g5ab[n, MID, i, pl.ds(sub, 1), :] = packed[4 * n + i : 4 * n + i + 1]
    abb = []
    for k, db in enumerate([s * d for d in range(MID, 0, -1) for s in (-1, 1)]):
        abb.append(
            remote(
                g5ab.at[:, MID, :, pl.ds(sub, 1), :],
                g5ab.at[:, MID - db, :, pl.ds(sub, 1), :],
                s_abb.at[k], r_abb.at[k], device(0, db),
            )
        )
    started += abb

    own[2].wait()
    for copy in p1:
        copy.wait_recv()

    def inside(start, shape, axis, count):
        at = lax.broadcasted_iota(jnp.int32, shape, axis) + start
        return (at >= 0) & (at < count)

    lanes3 = lax.broadcasted_iota(jnp.int32, (16, 256), 1)
    m3c = inside(N1 * b - 4, (16, 256), 0, N1 * NB)
    m3n = inside(N1 * b - 3, (16, 256), 0, N1 * NB)
    m3s = inside(N1 * b - 5, (16, 256), 0, N1 * NB)

    def row_in(r, size, origin):
        at = size * g + r - origin
        return jnp.where((at >= 0) & (at < size * NG), 1.0, 0.0).astype(F32)

    def table3(r, carry):
        here = row_in(r, N0, 4)
        bc = jnp.where(m3c, b3[r + 1, pl.ds(4, 16), :], 0.0) * here
        be = jnp.where(m3c, b3[r + 2, pl.ds(4, 16), :], 0.0) * row_in(r + 1, N0, 4)
        bw = jnp.where(m3c, b3[r, pl.ds(4, 16), :], 0.0) * row_in(r - 1, N0, 4)
        bn = jnp.where(m3n, b3[r + 1, pl.ds(5, 16), :], 0.0) * here
        bs = jnp.where(m3s, b3[r + 1, pl.ds(3, 16), :], 0.0) * here
        bu = jnp.where(lanes3 == 255, 0.0, pltpu.roll(bc, 255, 1))
        bd = jnp.where(lanes3 == 0, 0.0, pltpu.roll(bc, 1, 1))
        c = [0.5 * (bc + v) for v in (be, bw, bn, bs, bu, bd)]
        diag = a3[r] + c[0] + c[1] + c[2] + c[3] + c[4] + c[5]
        inv = jnp.where(m3c, 1.0 / diag, 0.0) * here
        for n in range(4):
            t3[n, r] = c[n] * inv
        t3[4, r] = jnp.where(lanes3 == 255, 0.0, c[4] * inv)
        t3[5, r] = jnp.where(lanes3 == 0, 0.0, c[5] * inv)
        d3[r] = diag
        fd = f3[r] * inv
        fd3[r] = fd
        x3b[r] = fd * (1.0 / smooth_middle)
        return carry

    smooth_middle, smooth_pairs = coefficients(SMOOTH, SMOOTH_LOW)
    lax.fori_loop(0, 24, table3, 0, unroll=4)

    def scaled_residual(t, fd, x, r):
        here = x[r]
        n, m = here.shape
        total = fd[r] - here
        total = total + t[0, r] * x[r + 1] + t[1, r] * x[r - 1]
        total = total + t[2, r] * pltpu.roll(here, n - 1, 0) + t[3, r] * pltpu.roll(here, 1, 0)
        return total + t[4, r] * pltpu.roll(here, m - 1, 1) + t[5, r] * pltpu.roll(here, 1, 1)

    def sweep(t, fd, now, old, lo, hi, chunk, pair):
        def rows(k, carry):
            for i in range(chunk):
                r = lo + k * chunk + i
                total = scaled_residual(t, fd, now, r)
                here = now[r]
                if len(pair) == 1:
                    old[r] = here + pair[0] * total
                else:
                    old[r] = here + pair[0] * (here - old[r]) + pair[1] * total
            return carry

        lax.fori_loop(0, (hi - lo) // chunk, rows, 0)

    sweep(t3, fd3, x3b, x3a, 1, 23, 11, smooth_pairs[0])
    sweep(t3, fd3, x3a, x3b, 2, 22, 10, smooth_pairs[1])
    sweep(t3, fd3, x3b, x3a, 3, 21, 9, smooth_pairs[2])

    def fine_residual(i):
        return d3[i] * scaled_residual(t3, fd3, x3a, i)

    for i in range(8):
        w3[i] = fine_residual(4 + 2 * i) + fine_residual(5 + 2 * i)
    f4[6:14, 6:10, :] = halve(w3[...], 4)
    f4_copies = []
    for k, (dg, db) in enumerate(FACES):
        f4_copies.append(
            halo(inner(f4, 6, 6), window(f4), dg, db, 4, 4, 6, 6, (8, 4), s_f4.at[k], r_f4.at[k])
        )
    started += f4_copies
    for i in range(16):
        h3[4 + i, 4:12, :] = x3a[4 + i, 4:12, :]
    x3_copies = []
    for k, (dg, db) in enumerate(FACES):
        x3_copies.append(
            halo(inner(h3, 4, 4), window(h3), dg, db, 4, 4, 4, 4, (N0, N1), s_x3.at[k], r_x3.at[k])
        )
    started += x3_copies

    for copy in abb:
        copy.wait_recv()
    aba = []
    for k, dg in enumerate((2, 4, 6)):
        aba.append(
            remote(
                g5ab.at[:, :, :, pl.ds(sub, 1), :], g5ab.at[:, :, :, pl.ds(sub, 1), :],
                s_aba.at[k], r_aba.at[k], device(dg, 0),
            )
        )
    started += aba

    for copy in ab4_copies:
        copy.wait_recv()
    lanes4 = lax.broadcasted_iota(jnp.int32, (16, 128), 1)
    m4 = inside(4 * b - 6, (16, 128), 0, 4 * NB)

    def masked4(r):
        return jnp.where(m4, ab4[1, r], 0.0) * row_in(r, 8, 6)

    def table4(r, carry):
        bc = masked4(r)
        be, bw = masked4(r + 1), masked4(r - 1)
        bn, bs = pltpu.roll(bc, 15, 0), pltpu.roll(bc, 1, 0)
        bu = jnp.where(lanes4 == 127, 0.0, pltpu.roll(bc, 127, 1))
        bd = jnp.where(lanes4 == 0, 0.0, pltpu.roll(bc, 1, 1))
        c = [0.125 * (bc + v) for v in (be, bw, bn, bs, bu, bd)]
        diag = ab4[0, r] + c[0] + c[1] + c[2] + c[3] + c[4] + c[5]
        inv = jnp.where(m4, 1.0 / diag, 0.0) * row_in(r, 8, 6)
        for n in range(4):
            t4[n, r] = c[n] * inv
        t4[4, r] = jnp.where(lanes4 == 127, 0.0, c[4] * inv)
        t4[5, r] = jnp.where(lanes4 == 0, 0.0, c[5] * inv)
        d4[r] = diag
        inv4[r] = inv
        return carry

    lax.fori_loop(1, 19, table4, 0, unroll=6)

    mine = pl.ds(pl.multiple_of(4 * core, 4), 4)
    partner = (g + 1 - 2 * core, b)
    for copy in aba:
        copy.wait_recv()
    abc = remote(
        g5ab.at[:, :, :, mine, :], g5ab.at[:, :, :, mine, :], s_abc.at[0], r_abc.at[0], partner
    )
    started.append(abc)

    for copy in f4_copies:
        copy.wait_recv()
    for r in range(2, 18):
        fd = f4[r] * inv4[r]
        fd4[r] = fd
        x4b[r] = fd * (1.0 / smooth_middle)
    sweep(t4, fd4, x4b, x4a, 3, 17, 14, smooth_pairs[0])
    sweep(t4, fd4, x4a, x4b, 4, 16, 12, smooth_pairs[1])
    sweep(t4, fd4, x4b, x4a, 5, 15, 10, smooth_pairs[2])

    for r in range(8):
        w4[r] = d4[6 + r] * scaled_residual(t4, fd4, x4a, 6 + r)
    pack(lambda r: w4[r, 6:10, :], 0)
    packed = 0.125 * dot(z5[...], gather)
    for i in range(4):
        g5f[MID, i, pl.ds(sub, 1), :] = packed[i : i + 1]
    fa = []
    for k, dg in enumerate((2, 4, 6)):
        fa.append(
            remote(
                g5f.at[MID, :, pl.ds(sub, 1), :], g5f.at[MID, :, pl.ds(sub, 1), :],
                s_fa.at[k], r_fa.at[k], device(dg, 0),
            )
        )
    started += fa

    p4[0, 6:14, 6:10, :] = f4[6:14, 6:10, :]
    p4[1, 6:14, 6:10, :] = x4a[6:14, 6:10, :]
    for copy in fa:
        copy.wait_recv()
    fb = []
    for k, db in enumerate([s * d for d in range(REACH, 0, -1) for s in (-1, 1)]):
        fb.append(
            remote(
                g5f.at[MID, :, mine, :], g5f.at[MID - db, :, mine, :],
                s_fb.at[k], r_fb.at[k], device(0, db),
            )
        )
    started += fb
    p4_copies = []
    for k, (dg, db) in enumerate(WIDE):
        p4_copies.append(
            halo(inner2(p4, 6, 6), window2(p4), dg, db, 6, 6, 6, 6, (8, 4), s_p4.at[k], r_p4.at[k])
        )
    started += p4_copies

    abc.wait_recv()
    lanes5 = lax.broadcasted_iota(jnp.int32, (8, 128), 1)
    subs5 = lax.broadcasted_iota(jnp.int32, (8, 128), 0)
    low = lanes5 < 64
    front = subs5 < 4
    up_end = (lanes5 == 63) | (lanes5 == 127)
    down_end = (lanes5 == 0) | (lanes5 == 64)

    def next_group(v):
        return jnp.where(front, pltpu.roll(v, 4, 0), pltpu.roll(v, 3, 0))

    def last_group(v):
        return jnp.where(front, pltpu.roll(v, 5, 0), pltpu.roll(v, 4, 0))

    def box_in(k):
        at = b + k - MID
        return jnp.where((at >= 0) & (at < NB), 1.0, 0.0).astype(F32)

    def beta5(k, i):
        return g5ab[1, k, i] * box_in(k)

    def table5(k, carry):
        bc = [beta5(k, i) for i in range(4)]
        half = [pltpu.roll(v, 64, 1) for v in bc]
        after = [pltpu.roll(beta5(k + 1, i), 64, 1) for i in range(4)]
        before = [pltpu.roll(beta5(k - 1, i), 64, 1) for i in range(4)]
        for i in range(4):
            be = bc[i + 1] if i < 3 else jnp.where(subs5 == 7, 0.0, next_group(bc[0]))
            bw = bc[i - 1] if i > 0 else jnp.where(subs5 == 0, 0.0, last_group(bc[3]))
            bn = jnp.where(low, half[i], after[i])
            bs = jnp.where(low, before[i], half[i])
            bu = jnp.where(up_end, 0.0, pltpu.roll(bc[i], 127, 1))
            bd = jnp.where(down_end, 0.0, pltpu.roll(bc[i], 1, 1))
            c = [0.03125 * (bc[i] + v) for v in (be, bw, bn, bs, bu, bd)]
            diag = g5ab[0, k, i] + c[0] + c[1] + c[2] + c[3] + c[4] + c[5]
            inv = box_in(k) / diag
            t5[0, k, i] = c[0] * inv if i < 3 else jnp.where(subs5 == 7, 0.0, c[0] * inv)
            t5[1, k, i] = c[1] * inv if i > 0 else jnp.where(subs5 == 0, 0.0, c[1] * inv)
            t5[2, k, i] = c[2] * inv
            t5[3, k, i] = c[3] * inv
            t5[4, k, i] = jnp.where(up_end, 0.0, c[4] * inv)
            t5[5, k, i] = jnp.where(down_end, 0.0, c[5] * inv)
            inv5[k, i] = inv
        return carry

    lax.fori_loop(1, SPAN - 1, table5, 0)

    for copy in fb:
        copy.wait_recv()
    fc = remote(
        g5f.at[pl.ds(1, SPAN - 2), :, mine, :], g5f.at[pl.ds(1, SPAN - 2), :, mine, :],
        s_fc.at[0], r_fc.at[0], partner,
    )
    started.append(fc)

    bottom_middle, bottom_pairs = coefficients(BOTTOM, BOTTOM_LOW)
    for m, (c1, c2) in enumerate(bottom_pairs):
        ends[m, 0] = F32(c1)
        ends[m, 1] = F32(c2)
    fc.wait_recv()
    for k in range(1, SPAN - 1):
        for i in range(4):
            fd = g5f[k, i] * inv5[k, i]
            fd5[k, i] = fd
            x5b[k, i] = fd * (1.0 / bottom_middle)

    def sweep5(now, old, reach, c1, c2):
        lo, hi = MID - reach, MID + reach + 1
        half = {}

        def turned(k, i):
            if (k, i) not in half:
                half[k, i] = pltpu.roll(now[k, i], 64, 1)
            return half[k, i]

        for k in range(lo, hi):
            x = [now[k, i] for i in range(4)]
            for i in range(4):
                east = x[i + 1] if i < 3 else next_group(x[0])
                west = x[i - 1] if i > 0 else last_group(x[3])
                north = jnp.where(low, turned(k, i), turned(k + 1, i))
                south = jnp.where(low, turned(k - 1, i), turned(k, i))
                total = fd5[k, i] - x[i]
                total = total + t5[0, k, i] * east + t5[1, k, i] * west
                total = total + t5[2, k, i] * north + t5[3, k, i] * south
                total = total + t5[4, k, i] * pltpu.roll(x[i], 127, 1) + t5[5, k, i] * pltpu.roll(x[i], 1, 1)
                old[k, i] = x[i] + c1 * (x[i] - old[k, i]) + c2 * total

    def two(reach, first):
        def body(k, carry):
            m = first + 2 * k
            sweep5(x5b, x5a, reach, ends[m, 0], ends[m, 1])
            sweep5(x5a, x5b, reach, ends[m + 1, 0], ends[m + 1, 1])
            return carry

        return body

    lax.fori_loop(0, 2, two(9, 0), 0)
    lax.fori_loop(0, 2, two(7, 4), 0)
    lax.fori_loop(0, 2, two(5, 8), 0)
    two(3, 12)(0, 0)
    sweep5(x5b, x5a, 2, ends[14, 0], ends[14, 1])

    for a in range(10):
        row = a - 3
        group = lax.rem(g + (row // 4) + NG, NG)
        at = 4 * lax.rem(group, 2) + group // 2
        for k in range(5):
            line = x5a[MID - 2 + k, row % 4, pl.ds(at, 1), :]
            first, last = max(4 * k - 2, 0), min(4 * k + 2, 16)
            q4[a, first:last, :] = jnp.broadcast_to(line, (last - first, 128))
    grown = dot(q4[...].reshape(160, 128), spread).reshape(10, 16, 256)
    rows4 = lax.broadcasted_iota(jnp.int32, (16, 128), 0)
    first_of_box = lax.rem(lax.shift_right_logical(rows4 + 2, 1), 2) == 0
    for copy in p4_copies:
        copy.wait_recv()
    for a in range(10):
        line = jnp.where(first_of_box, grown[a, :, 0:128], grown[a, :, 128:256])
        for r in (2 * a, 2 * a + 1):
            x4b[r] = jnp.where(m4, p4[1, r] + line, 0.0) * row_in(r, 8, 6)
            if 1 <= r < 19:
                fd4[r] = p4[0, r] * inv4[r]
    sweep(t4, fd4, x4b, x4a, 1, 19, 18, (1.0 / smooth_middle,))
    sweep(t4, fd4, x4a, x4b, 2, 18, 16, smooth_pairs[0])
    sweep(t4, fd4, x4b, x4a, 3, 17, 14, smooth_pairs[1])
    sweep(t4, fd4, x4a, x4b, 4, 16, 12, smooth_pairs[2])

    grown = dot(x4b[4:16, 4:12, :].reshape(96, 128), spread).reshape(12, 8, 256)
    for r in range(12):
        for k in range(2):
            line = grown[r, :, 128 * k : 128 * k + 128]
            u4[k, r, pl.ds(0, 8, stride=2), :] = line
            u4[k, r, pl.ds(1, 8, stride=2), :] = line
    for copy in x3_copies:
        copy.wait_recv()
    for r in range(24):
        row = row_in(r, N0, 4)
        for k in range(2):
            lanes = slice(128 * k, 128 * k + 128)
            x3b[r, :, lanes] = jnp.where(m3c[:, lanes], (h3[r, :, lanes] + u4[k, r // 2]) * row, 0.0)
    sweep(t3, fd3, x3b, x3a, 1, 23, 11, (1.0 / smooth_middle,))
    sweep(t3, fd3, x3a, x3b, 2, 22, 10, smooth_pairs[0])
    sweep(t3, fd3, x3b, x3a, 3, 21, 9, smooth_pairs[1])
    sweep(t3, fd3, x3a, x3b, 4, 20, 8, smooth_pairs[2])
    result = pltpu.make_async_copy(x3b.at[pl.ds(4, N0), pl.ds(4, N1), :], out, own_sem.at[0])
    result.start()
    for copy in started:
        copy.wait_send()
    result.wait()


SCRATCH = (
    [pltpu.VMEM(shape, F32) for shape in (
        (24, 16, 256), (24, 16, 256), (26, 24, 256), (6, 24, 16, 256), (24, 16, 256), (24, 16, 256),
        (24, 16, 256), (24, 16, 256), (24, 16, 256),
        (2, 20, 16, 128), (20, 16, 128), (2, 20, 16, 128), (6, 20, 16, 128), (20, 16, 128), (20, 16, 128),
        (20, 16, 128), (20, 16, 128), (20, 16, 128), (8, 16, 128),
        (8, 256), (2, SPAN, 4, 8, 128), (SPAN, 4, 8, 128), (6, SPAN, 4, 8, 128), (SPAN, 4, 8, 128),
        (SPAN, 4, 8, 128), (SPAN, 4, 8, 128), (SPAN, 4, 8, 128), (10, 16, 128), (8, 16, 256),
        (2, 12, 16, 128),
    )]
    + [pltpu.SemaphoreType.DMA((3,)), pltpu.SMEM((16, 2), F32)]
    + [pltpu.SemaphoreType.DMA(shape) for count in (
        (3, 8), (14,), (8,), (8,), (14,), (3,), (2 * MID,), (1,), (3,), (2 * REACH,), (1,)
    ) for shape in (count, count)]
)


def cycle(source, alpha, beta):
    return pl.pallas_call(
        kernel,
        out_shape=jax.ShapeDtypeStruct((N0, N1, N2), F32),
        in_specs=[pl.BlockSpec(memory_space=pl.ANY)] * 3,
        out_specs=pl.BlockSpec(memory_space=pl.ANY),
        scratch_shapes=SCRATCH,
        compiler_params=pltpu.CompilerParams(
            collective_id=0, has_side_effects=True, vmem_limit_bytes=48 << 20
        ),
        name="vcycle",
    )(source, alpha, beta)


def solution(mesh):
    spec = P("grp", "box", None)
    return jax.shard_map(cycle, mesh=mesh, in_specs=(spec,) * 3, out_specs=spec, check_vma=False)
```

time: 542 us -> 56.8 us (0.10); the launches traced: 536 us -> 56.7 us
  starting transfers between devices: 261 us -> 0 us
  waiting for transfers between devices: 117 us -> 0 us
  local copies, waits for them, and re-layouts: 66.4 us -> 3.37 us
  Pallas kernels: 0 us -> 53.3 us
  other arithmetic: 50 us -> 0 us
  blocking collectives: 39.1 us -> 0 us
    ppermute x86 -> x0, starting transfers between devices: 261 us -> none  [the longest x43 200 us: padded_2(): lax.ppermute(tail, axis, [(i, (i + 1) % count) for i in range(ends)])]
    ppermute x86 -> x0, waiting for transfers between devices: 117 us -> none  [the longest x43 117 us: padded_2(): lax.ppermute(head, axis, [((i + 1) % count, i) for i in range(ends)])]
    reshape x9 -> x0, local copies, waits for them, and re-layouts: 60.8 us -> none  [the longest x6 60.2 us: restrict(): field.reshape(sizes[0] // 2, 2, sizes[1] // 2, 2, sizes[2] // 2, 2)]
    pallas_call x0 -> x1, Pallas kernels: none -> 53.3 us  [cycle(): pl.pallas_call(kernel, out_shape=jax.ShapeDtypeStruct((N0, N1, N2), F32),...]
    all_gather x3 -> x0, blocking collectives: 39.1 us -> none  [the longest x1 14.1 us: shards(): lax.all_gather(local_four, 'grp', axis=0, tiled=True)]
    reduce_sum x6 -> x0, other arithmetic: 24.4 us -> none  [restrict(): field.reshape(sizes[0] // 2, 2, sizes[1] // 2, 2, sizes[2] // 2, 2)]
    add x32 -> x0, other arithmetic: 14.1 us -> none  [the longest x29 13 us: chebyshev(): approx = approx + update]
    concatenate x42 -> x0, other arithmetic: 7.77 us -> none  [padded_2(): jnp.concatenate([lax.ppermute(tail, axis, [(i, (i + 1) % count) for i in...]
  transfers between devices with their start and end apart: 86 -> 0, of which waited for: 35 -> 0; matrix products, arithmetic and copies ran while one was open for 12% -> 0% of each run, Pallas kernels for 0% -> 0%
where the time goes in v1:
time: 56.8 us; the launch traced here: 56.7 us
  Pallas kernels  53.3 us (94%)
  local copies, waits for them, and re-layouts  3.37 us (6%)
    pallas_call x1, Pallas kernels, cycle(): pl.pallas_call(kernel, out_shape=jax.ShapeDtypeStruct((N0, N1, N2), F32),...  53.3 us
    unnamed x7, local copies, waits for them, and re-layouts  3.37 us

profile of v1, /device:TPU:1, one launch (start us, length us, event | category | flops | bytes accessed | tf_op | source)
XLA Modules:
  0.0 56.7 jit_solution(9966249682822010706)
XLA Ops:
  0.0 0.0 copy-start
  0.0 0.9 %copy-done = f32[16,8,256]{2,1,0:T(8,128)S(1)} copy-done((f32[16,8,256]{2,1,0:T(8,128)S(1)}, f32[16,8,256]{2,1,0:T(8,128)}, u32[]{:S(2)}) %copy-start) | copy-done | bytes 131096
  0.9 0.0 copy-start.1
  0.9 0.9 %copy-done.1 = f32[16,8,256]{2,1,0:T(8,128)S(1)} copy-done((f32[16,8,256]{2,1,0:T(8,128)S(1)}, f32[16,8,256]{2,1,0:T(8,128)}, u32[]{:S(2)}) %copy-start.1) | copy-done | bytes 131096
  1.8 0.0 copy-start.2
  1.8 0.9 %copy-done.2 = f32[16,8,256]{2,1,0:T(8,128)S(1)} copy-done((f32[16,8,256]{2,1,0:T(8,128)S(1)}, f32[16,8,256]{2,1,0:T(8,128)}, u32[]{:S(2)}) %copy-start.2) | copy-done | bytes 131096
  2.7 53.3 %vcycle.1 = f32[16,8,256]{2,1,0:T(8,128)S(1)} custom-call(f32[16,8,256]{2,1,0:T(8,128)S(1)} %copy-done, f32[16,8,256]{2,1,0:T(8,128)S(1)} %copy-done.1, f32[16,8,256]{2,1,0:T(8,128)S(1)} %copy-done.2), custom_call_target="tpu_custom_call" | custom-call | tf_op jit(solution)/shard_map/vcycle/pallas_call | solution.py:534
  56.1 0.7 %copy.5 = f32[16,8,256]{2,1,0:T(8,128)} copy(f32[16,8,256]{2,1,0:T(8,128)S(1)} %vcycle.1) | data formatting | bytes 262144
Async XLA Ops:
  0.0 0.9 %copy-start = (f32[16,8,256]{2,1,0:T(8,128)S(1)}, f32[16,8,256]{2,1,0:T(8,128)}, u32[]{:S(2)}) copy-start(f32[16,8,256]{2,1,0:T(8,128)} %source.1) | copy-start | bytes 393220
  0.9 0.9 %copy-start.1 = (f32[16,8,256]{2,1,0:T(8,128)S(1)}, f32[16,8,256]{2,1,0:T(8,128)}, u32[]{:S(2)}) copy-start(f32[16,8,256]{2,1,0:T(8,128)} %alpha.1) | copy-start | bytes 393220
  1.8 0.9 %copy-start.2 = (f32[16,8,256]{2,1,0:T(8,128)S(1)}, f32[16,8,256]{2,1,0:T(8,128)}, u32[]{:S(2)}) copy-start(f32[16,8,256]{2,1,0:T(8,128)} %beta.1) | copy-start | bytes 393220

commit v2 on v1

--- a/solution.py
+++ b/solution.py
@@ -20,7 +20,6 @@
 SPAN = 2 * MID + 1
 
 FACES = [(dg, db) for db in (-1, 1, 0) for dg in (0, -1, 1) if (dg, db) != (0, 0)]
-WIDE = [(dg, db) for db in (-2, 2, -1, 1, 0) for dg in (0, -1, 1) if (dg, db) != (0, 0)]
 
 
 def coefficients(degree, lower):
@@ -84,17 +83,12 @@
 
     f4[...] = jnp.zeros_like(f4)
 
-    partners = set(FACES) | set(WIDE) | {(2, 0), (4, 0), (6, 0)}
+    partners = set(FACES) | {(2, 0), (4, 0), (6, 0)}
     partners |= {(0, k) for k in range(-MID, MID + 1) if k}
     partners = sorted(partners, key=lambda p: -abs(p[1]))
     barrier = pltpu.get_barrier_semaphore()
     for dg, db in partners:
         pl.semaphore_signal(barrier, inc=1, device_id=device(dg, db), device_id_type=MESH)
-
-    x3a[...] = jnp.zeros_like(x3a)
-    x4a[...] = jnp.zeros_like(x4a)
-    x5a[...] = jnp.zeros_like(x5a)
-    x5b[...] = jnp.zeros_like(x5b)
 
     pl.semaphore_wait(barrier, len(partners))
 
@@ -156,12 +150,6 @@
     ab4[1, 6:14, 6:10, :] = halve(
         jnp.stack([b3[5 + 2 * i, 8:16, :] + b3[6 + 2 * i, 8:16, :] for i in range(8)]), 0
     )
-    ab4_copies = []
-    for k, (dg, db) in enumerate(WIDE):
-        ab4_copies.append(
-            halo(inner2(ab4, 6, 6), window2(ab4), dg, db, 6, 6, 6, 6, (8, 4), s_ab4.at[k], r_ab4.at[k])
-        )
-    started += ab4_copies
     for n in range(2):
         pack(lambda r, n=n: ab4[n, 6 + r, 6:10, :], 4 * n)
     packed = 0.125 * dot(z5[...], gather)
@@ -178,6 +166,33 @@
             )
         )
     started += abb
+
+    def boxes4(ref, send, recv):
+        copies = []
+        for k, db in enumerate((-2, 2, -1, 1)):
+            copies.append(
+                halo(inner2(ref, 6, 6), window2(ref), 0, db, 6, 6, 6, 6, (8, 4), send.at[k], recv.at[k])
+            )
+        return copies
+
+    def groups4(ref, send, recv):
+        copies = []
+        for k, dg in enumerate((-1, 1)):
+            s0, t0, l0 = part(dg, 8, 6, 6)
+            copies.append(
+                remote(
+                    ref.at[:, pl.ds(6 + s0, l0)], ref.at[:, pl.ds(t0, l0)],
+                    send.at[4 + k], recv.at[4 + k], device(dg, 0),
+                )
+            )
+        return copies
+
+    ab4_boxes = boxes4(ab4, s_ab4, r_ab4)
+    started += ab4_boxes
+
+    x4a[...] = jnp.zeros_like(x4a)
+    x5a[...] = jnp.zeros_like(x5a)
+    x5b[...] = jnp.zeros_like(x5b)
 
     own[2].wait()
     for copy in p1:
@@ -216,6 +231,7 @@
         fd = f3[r] * inv
         fd3[r] = fd
         x3b[r] = fd * (1.0 / smooth_middle)
+        x3a[r] = jnp.zeros_like(fd)
         return carry
 
     smooth_middle, smooth_pairs = coefficients(SMOOTH, SMOOTH_LOW)
@@ -262,9 +278,13 @@
     for i in range(16):
         h3[4 + i, 4:12, :] = x3a[4 + i, 4:12, :]
     x3_copies = []
-    for k, (dg, db) in enumerate(FACES):
+    for copy in ab4_boxes:
+        copy.wait_recv()
+    ab4_groups = groups4(ab4, s_ab4, r_ab4)
+    started += ab4_groups
+    for k, db in enumerate((-1, 1)):
         x3_copies.append(
-            halo(inner(h3, 4, 4), window(h3), dg, db, 4, 4, 4, 4, (N0, N1), s_x3.at[k], r_x3.at[k])
+            halo(inner(h3, 4, 4), window(h3), 0, db, 4, 4, 4, 4, (N0, N1), s_x3.at[k], r_x3.at[k])
         )
     started += x3_copies
 
@@ -280,7 +300,7 @@
         )
     started += aba
 
-    for copy in ab4_copies:
+    for copy in ab4_groups:
         copy.wait_recv()
     lanes4 = lax.broadcasted_iota(jnp.int32, (16, 128), 1)
     m4 = inside(4 * b - 6, (16, 128), 0, 4 * NB)
@@ -309,12 +329,6 @@
 
     mine = pl.ds(pl.multiple_of(4 * core, 4), 4)
     partner = (g + 1 - 2 * core, b)
-    for copy in aba:
-        copy.wait_recv()
-    abc = remote(
-        g5ab.at[:, :, :, mine, :], g5ab.at[:, :, :, mine, :], s_abc.at[0], r_abc.at[0], partner
-    )
-    started.append(abc)
 
     for copy in f4_copies:
         copy.wait_recv()
@@ -342,6 +356,26 @@
         )
     started += fa
 
+    for copy in aba:
+        copy.wait_recv()
+    abc = remote(
+        g5ab.at[:, :, :, mine, :], g5ab.at[:, :, :, mine, :], s_abc.at[0], r_abc.at[0], partner
+    )
+    started.append(abc)
+
+    for copy in x3_copies:
+        copy.wait_recv()
+    x3_groups = []
+    for k, dg in enumerate((-1, 1)):
+        s0, t0, l0 = part(dg, N0, 4, 4)
+        x3_groups.append(
+            remote(
+                h3.at[pl.ds(4 + s0, l0)], h3.at[pl.ds(t0, l0)],
+                s_x3.at[2 + k], r_x3.at[2 + k], device(dg, 0),
+            )
+        )
+    started += x3_groups
+
     p4[0, 6:14, 6:10, :] = f4[6:14, 6:10, :]
     p4[1, 6:14, 6:10, :] = x4a[6:14, 6:10, :]
     for copy in fa:
@@ -355,12 +389,8 @@
             )
         )
     started += fb
-    p4_copies = []
-    for k, (dg, db) in enumerate(WIDE):
-        p4_copies.append(
-            halo(inner2(p4, 6, 6), window2(p4), dg, db, 6, 6, 6, 6, (8, 4), s_p4.at[k], r_p4.at[k])
-        )
-    started += p4_copies
+    p4_boxes = boxes4(p4, s_p4, r_p4)
+    started += p4_boxes
 
     abc.wait_recv()
     lanes5 = lax.broadcasted_iota(jnp.int32, (8, 128), 1)
@@ -416,6 +446,10 @@
         s_fc.at[0], r_fc.at[0], partner,
     )
     started.append(fc)
+    for copy in p4_boxes:
+        copy.wait_recv()
+    p4_groups = groups4(p4, s_p4, r_p4)
+    started += p4_groups
 
     bottom_middle, bottom_pairs = coefficients(BOTTOM, BOTTOM_LOW)
     for m, (c1, c2) in enumerate(bottom_pairs):
@@ -476,7 +510,7 @@
     grown = dot(q4[...].reshape(160, 128), spread).reshape(10, 16, 256)
     rows4 = lax.broadcasted_iota(jnp.int32, (16, 128), 0)
     first_of_box = lax.rem(lax.shift_right_logical(rows4 + 2, 1), 2) == 0
-    for copy in p4_copies:
+    for copy in p4_groups:
         copy.wait_recv()
     for a in range(10):
         line = jnp.where(first_of_box, grown[a, :, 0:128], grown[a, :, 128:256])
@@ -495,7 +529,7 @@
             line = grown[r, :, 128 * k : 128 * k + 128]
             u4[k, r, pl.ds(0, 8, stride=2), :] = line
             u4[k, r, pl.ds(1, 8, stride=2), :] = line
-    for copy in x3_copies:
+    for copy in x3_groups:
         copy.wait_recv()
     for r in range(24):
         row = row_in(r, N0, 4)
@@ -525,7 +559,7 @@
     )]
     + [pltpu.SemaphoreType.DMA((3,)), pltpu.SMEM((16, 2), F32)]
     + [pltpu.SemaphoreType.DMA(shape) for count in (
-        (3, 8), (14,), (8,), (8,), (14,), (3,), (2 * MID,), (1,), (3,), (2 * REACH,), (1,)
+        (3, 8), (6,), (8,), (4,), (6,), (3,), (2 * MID,), (1,), (3,), (2 * REACH,), (1,)
     ) for shape in (count, count)]
 )
 
@@ -538,7 +572,7 @@
         out_specs=pl.BlockSpec(memory_space=pl.ANY),
         scratch_shapes=SCRATCH,
         compiler_params=pltpu.CompilerParams(
-            collective_id=0, has_side_effects=True, vmem_limit_bytes=48 << 20
+            collective_id=0, has_side_effects=True, vmem_limit_bytes=63 << 20
         ),
         name="vcycle",
     )(source, alpha, beta)

time: 56.8 us -> 52.1 us (0.917)
  Pallas kernels: 53.3 us -> 50.4 us
  local copies, waits for them, and re-layouts: 3.37 us -> 1.57 us
    pallas_call x1, Pallas kernels: 53.3 us -> 50.4 us  [cycle(): pl.pallas_call(kernel, out_shape=jax.ShapeDtypeStruct((N0, N1, N2), F32),...]
    unnamed x7 -> x1, local copies, waits for them, and re-layouts: 3.37 us -> 1.57 us
where the time goes in v2:
time: 52.1 us; the launch traced here: 52 us
  Pallas kernels  50.4 us (97%)
  local copies, waits for them, and re-layouts  1.57 us (3%)
    pallas_call x1, Pallas kernels, cycle(): pl.pallas_call(kernel, out_shape=jax.ShapeDtypeStruct((N0, N1, N2), F32),...  50.4 us
    unnamed x1, local copies, waits for them, and re-layouts  1.57 us

profile of v2, /device:TPU:1, one launch (start us, length us, event | category | flops | bytes accessed | tf_op | source)
XLA Modules:
  0.0 52.0 jit_solution(4842162581763560593)
XLA Ops:
  0.0 50.4 %vcycle.1 = f32[16,8,256]{2,1,0:T(8,128)} custom-call(f32[16,8,256]{2,1,0:T(8,128)} %source.1, f32[16,8,256]{2,1,0:T(8,128)} %alpha.1, f32[16,8,256]{2,1,0:T(8,128)} %beta.1), custom_call_target="tpu_custom_call" | custom-call | tf_op jit(solution)/shard_map/vcycle/pallas_call | solution.py:568
  50.4 1.6 %copy.5 = f32[16,8,256]{2,1,0:T(8,128)} copy(f32[16,8,256]{2,1,0:T(8,128)} %vcycle.1) | data formatting | bytes 262144

commit v3 on v2

--- a/solution.py
+++ b/solution.py
@@ -53,7 +53,7 @@
     f3, a3, b3, t3, d3, fd3, x3a, x3b, h3,
     ab4, f4, p4, t4, inv4, d4, fd4, x4a, x4b, w4,
     z5, g5ab, g5f, t5, inv5, fd5, x5a, x5b, q4, w3, u4,
-    own_sem, ends,
+    own_sem, hello, ends,
     s_p1, r_p1, s_ab4, r_ab4, s_f4, r_f4, s_x3, r_x3, s_p4, r_p4,
     s_aba, r_aba, s_abb, r_abb, s_abc, r_abc, s_fa, r_fa, s_fb, r_fb, s_fc, r_fc,
 ):
@@ -83,9 +83,7 @@
 
     f4[...] = jnp.zeros_like(f4)
 
-    partners = set(FACES) | {(2, 0), (4, 0), (6, 0)}
-    partners |= {(0, k) for k in range(-MID, MID + 1) if k}
-    partners = sorted(partners, key=lambda p: -abs(p[1]))
+    partners = FACES + [(0, -8), (0, 8)]
     barrier = pltpu.get_barrier_semaphore()
     for dg, db in partners:
         pl.semaphore_signal(barrier, inc=1, device_id=device(dg, db), device_id_type=MESH)
@@ -120,6 +118,12 @@
                 halo(window(src), window(dst), dg, db, w, w, o0, o1, (N0, N1), s_p1.at[n, k], r_p1.at[n, k])
             )
     started += p1
+
+    def greet(n, peers):
+        for dg, db in peers:
+            pl.semaphore_signal(hello.at[n], inc=1, device_id=device(dg, db), device_id_type=MESH)
+
+    greet(0, ((0, -1), (0, 1), (-1, 0), (1, 0)))
 
     rows256 = lax.broadcasted_iota(jnp.int32, (256, 128), 0)
     cols128 = lax.broadcasted_iota(jnp.int32, (256, 128), 1)
@@ -150,12 +154,15 @@
     ab4[1, 6:14, 6:10, :] = halve(
         jnp.stack([b3[5 + 2 * i, 8:16, :] + b3[6 + 2 * i, 8:16, :] for i in range(8)]), 0
     )
+    pl.semaphore_wait(hello.at[0], 4)
+    greet(1, ((0, -2), (0, 2), (-2, 0), (2, 0)))
     for n in range(2):
         pack(lambda r, n=n: ab4[n, 6 + r, 6:10, :], 4 * n)
     packed = 0.125 * dot(z5[...], gather)
     for n in range(2):
         for i in range(4):
             g5ab[n, MID, i, pl.ds(sub, 1), :] = packed[4 * n + i : 4 * n + i + 1]
+    pl.semaphore_wait(hello.at[1], 4)
     abb = []
     for k, db in enumerate([s * d for d in range(MID, 0, -1) for s in (-1, 1)]):
         abb.append(
@@ -194,8 +201,7 @@
     x5a[...] = jnp.zeros_like(x5a)
     x5b[...] = jnp.zeros_like(x5b)
 
-    own[2].wait()
-    for copy in p1:
+    for copy in p1[:16]:
         copy.wait_recv()
 
     def inside(start, shape, axis, count):
@@ -228,7 +234,11 @@
         t3[4, r] = jnp.where(lanes3 == 255, 0.0, c[4] * inv)
         t3[5, r] = jnp.where(lanes3 == 0, 0.0, c[5] * inv)
         d3[r] = diag
-        fd = f3[r] * inv
+        fd3[r] = inv
+        return carry
+
+    def start3(r, carry):
+        fd = f3[r] * fd3[r]
         fd3[r] = fd
         x3b[r] = fd * (1.0 / smooth_middle)
         x3a[r] = jnp.zeros_like(fd)
@@ -236,6 +246,10 @@
 
     smooth_middle, smooth_pairs = coefficients(SMOOTH, SMOOTH_LOW)
     lax.fori_loop(0, 24, table3, 0, unroll=4)
+    own[2].wait()
+    for copy in p1[16:]:
+        copy.wait_recv()
+    lax.fori_loop(0, 24, start3, 0, unroll=8)
 
     def scaled_residual(t, fd, x, r):
         here = x[r]
@@ -381,7 +395,8 @@
     for copy in fa:
         copy.wait_recv()
     fb = []
-    for k, db in enumerate([s * d for d in range(REACH, 0, -1) for s in (-1, 1)]):
+    fb_from = [s * d for d in range(REACH, 0, -1) for s in (-1, 1)]
+    for k, db in enumerate(fb_from):
         fb.append(
             remote(
                 g5f.at[MID, :, mine, :], g5f.at[MID - db, :, mine, :],
@@ -438,14 +453,20 @@
         return carry
 
     lax.fori_loop(1, SPAN - 1, table5, 0)
-
-    for copy in fb:
-        copy.wait_recv()
-    fc = remote(
-        g5f.at[pl.ds(1, SPAN - 2), :, mine, :], g5f.at[pl.ds(1, SPAN - 2), :, mine, :],
-        s_fc.at[0], r_fc.at[0], partner,
-    )
-    started.append(fc)
+    for copy in started:
+        copy.wait_send()
+    started = []
+
+    fc = []
+    for k, (first, last) in enumerate(((MID - 3, MID + 3), (1, MID - 4), (MID + 4, SPAN - 2))):
+        for copy, db in zip(fb, fb_from):
+            if first <= MID - db <= last:
+                copy.wait_recv()
+        span = pl.ds(first, last - first + 1)
+        fc.append(
+            remote(g5f.at[span, :, mine, :], g5f.at[span, :, mine, :], s_fc.at[k], r_fc.at[k], partner)
+        )
+    started += fc
     for copy in p4_boxes:
         copy.wait_recv()
     p4_groups = groups4(p4, s_p4, r_p4)
@@ -455,7 +476,8 @@
     for m, (c1, c2) in enumerate(bottom_pairs):
         ends[m, 0] = F32(c1)
         ends[m, 1] = F32(c2)
-    fc.wait_recv()
+    for copy in fc:
+        copy.wait_recv()
     for k in range(1, SPAN - 1):
         for i in range(4):
             fd = g5f[k, i] * inv5[k, i]
@@ -488,7 +510,7 @@
         def body(k, carry):
             m = first + 2 * k
             sweep5(x5b, x5a, reach, ends[m, 0], ends[m, 1])
-            sweep5(x5a, x5b, reach, ends[m + 1, 0], ends[m + 1, 1])
+            sweep5(x5a, x5b, reach - 1, ends[m + 1, 0], ends[m + 1, 1])
             return carry
 
         return body
@@ -557,9 +579,9 @@
         (SPAN, 4, 8, 128), (SPAN, 4, 8, 128), (SPAN, 4, 8, 128), (10, 16, 128), (8, 16, 256),
         (2, 12, 16, 128),
     )]
-    + [pltpu.SemaphoreType.DMA((3,)), pltpu.SMEM((16, 2), F32)]
+    + [pltpu.SemaphoreType.DMA((3,)), pltpu.SemaphoreType.REGULAR((2,)), pltpu.SMEM((16, 2), F32)]
     + [pltpu.SemaphoreType.DMA(shape) for count in (
-        (3, 8), (6,), (8,), (4,), (6,), (3,), (2 * MID,), (1,), (3,), (2 * REACH,), (1,)
+        (3, 8), (6,), (8,), (4,), (6,), (3,), (2 * MID,), (1,), (3,), (2 * REACH,), (3,)
     ) for shape in (count, count)]
 )
 

time: 52.1 us -> 50.9 us (0.977)
  Pallas kernels: 50.4 us -> 49.2 us
    pallas_call x1, Pallas kernels: 50.4 us -> 49.2 us  [cycle(): pl.pallas_call(kernel, out_shape=jax.ShapeDtypeStruct((N0, N1, N2), F32),...]
where the time goes in v3:
time: 50.9 us; the launch traced here: 50.8 us
  Pallas kernels  49.2 us (97%)
  local copies, waits for them, and re-layouts  1.57 us (3%)
    pallas_call x1, Pallas kernels, cycle(): pl.pallas_call(kernel, out_shape=jax.ShapeDtypeStruct((N0, N1, N2), F32),...  49.2 us
    unnamed x1, local copies, waits for them, and re-layouts  1.57 us

profile of v3, /device:TPU:1, one launch (start us, length us, event | category | flops | bytes accessed | tf_op | source)
XLA Modules:
  0.0 50.8 jit_solution(12713968327385631671)
XLA Ops:
  0.0 49.2 %vcycle.1 = f32[16,8,256]{2,1,0:T(8,128)} custom-call(f32[16,8,256]{2,1,0:T(8,128)} %source.1, f32[16,8,256]{2,1,0:T(8,128)} %alpha.1, f32[16,8,256]{2,1,0:T(8,128)} %beta.1), custom_call_target="tpu_custom_call" | custom-call | tf_op jit(solution)/shard_map/vcycle/pallas_call | solution.py:590
  49.2 1.6 %copy.5 = f32[16,8,256]{2,1,0:T(8,128)} copy(f32[16,8,256]{2,1,0:T(8,128)} %vcycle.1) | data formatting | bytes 262144

commit v4 on v3

--- a/solution.py
+++ b/solution.py
@@ -50,11 +50,11 @@
 
 def kernel(
     source, alpha, beta, out,
-    f3, a3, b3, t3, d3, fd3, x3a, x3b, h3,
+    bo, af, to, fdo, xo, xr, lb, lz, f3, a3, b3, t3, d3, fd3, x3a, x3b, h3,
     ab4, f4, p4, t4, inv4, d4, fd4, x4a, x4b, w4,
     z5, g5ab, g5f, t5, inv5, fd5, x5a, x5b, q4, w3, u4,
     own_sem, hello, ends,
-    s_p1, r_p1, s_ab4, r_ab4, s_f4, r_f4, s_x3, r_x3, s_p4, r_p4,
+    s_p1, r_p1, s_x12, r_x12, s_late, r_late, s_ab4, r_ab4, s_f4, r_f4, s_x3, r_x3, s_p4, r_p4,
     s_aba, r_aba, s_abb, r_abb, s_abc, r_abc, s_fa, r_fa, s_fb, r_fb, s_fc, r_fc,
 ):
     g, b = lax.axis_index("grp"), lax.axis_index("box")
@@ -74,9 +74,9 @@
     started = []
 
     own = [
-        pltpu.make_async_copy(beta, b3.at[pl.ds(5, N0), pl.ds(8, N1), :], own_sem.at[0]),
-        pltpu.make_async_copy(alpha, a3.at[pl.ds(4, N0), pl.ds(4, N1), :], own_sem.at[1]),
-        pltpu.make_async_copy(source, f3.at[pl.ds(4, N0), pl.ds(4, N1), :], own_sem.at[2]),
+        pltpu.make_async_copy(beta, bo.at[pl.ds(5, N0)], own_sem.at[0]),
+        pltpu.make_async_copy(alpha, af.at[0, pl.ds(4, N0)], own_sem.at[1]),
+        pltpu.make_async_copy(source, af.at[1, pl.ds(4, N0)], own_sem.at[2]),
     ]
     for copy in own:
         copy.start()
@@ -109,13 +109,26 @@
     def inner2(ref, o0, o1):
         return lambda i, n, j, m: ref.at[:, pl.ds(o0 + i, n), pl.ds(o1 + j, m), :]
 
+    along = []
+    for n, (src, dst, w, o0) in enumerate(
+        ((beta, bo, 5, 5), (alpha, af.at[0], 4, 4), (source, af.at[1], 4, 4))
+    ):
+        for k, dg in enumerate((-1, 1)):
+            s0, t0, l0 = part(dg, N0, w, o0)
+            along.append(
+                remote(src.at[pl.ds(s0, l0)], dst.at[pl.ds(t0, l0)], s_p1.at[n, k], r_p1.at[n, k], device(dg, 0))
+            )
+    started += along
     p1 = []
-    for n, (src, dst, w, o0, o1) in enumerate(
-        ((beta, b3, 5, 5, 8), (alpha, a3, 4, 4, 4), (source, f3, 4, 4, 4))
+    for n, (src, dst, w0, w1, o0, o1) in enumerate(
+        ((beta, b3, 5, 3, 5, 8), (alpha, a3, 4, 2, 4, 4), (source, f3, 4, 2, 4, 4))
     ):
-        for k, (dg, db) in enumerate(FACES):
+        for k, (dg, db) in enumerate(FACES[:6]):
             p1.append(
-                halo(window(src), window(dst), dg, db, w, w, o0, o1, (N0, N1), s_p1.at[n, k], r_p1.at[n, k])
+                halo(
+                    window(src), window(dst), dg, db, w0, w1, o0, o1, (N0, N1),
+                    s_p1.at[n, 2 + k], r_p1.at[n, 2 + k],
+                )
             )
     started += p1
 
@@ -149,13 +162,74 @@
     for copy in own[:2]:
         copy.wait()
     ab4[0, 6:14, 6:10, :] = halve(
-        jnp.stack([a3[4 + 2 * i, 4:12, :] + a3[5 + 2 * i, 4:12, :] for i in range(8)]), 0
+        jnp.stack([af[0, 4 + 2 * i] + af[0, 5 + 2 * i] for i in range(8)]), 0
     )
     ab4[1, 6:14, 6:10, :] = halve(
-        jnp.stack([b3[5 + 2 * i, 8:16, :] + b3[6 + 2 * i, 8:16, :] for i in range(8)]), 0
+        jnp.stack([bo[5 + 2 * i] + bo[6 + 2 * i] for i in range(8)]), 0
     )
     pl.semaphore_wait(hello.at[0], 4)
     greet(1, ((0, -2), (0, 2), (-2, 0), (2, 0)))
+    def inside(start, shape, axis, count):
+        at = lax.broadcasted_iota(jnp.int32, shape, axis) + start
+        return (at >= 0) & (at < count)
+
+    def row_in(r, size, origin):
+        at = size * g + r - origin
+        return jnp.where((at >= 0) & (at < size * NG), 1.0, 0.0).astype(F32)
+
+    lanes3 = lax.broadcasted_iota(jnp.int32, (16, 256), 1)
+    smooth_middle, smooth_pairs = coefficients(SMOOTH, SMOOTH_LOW)
+
+    def scaled_residual(t, fd, x, r):
+        here = x[r]
+        n, m = here.shape
+        total = fd[r] - here
+        total = total + t[0, r] * x[r + 1] + t[1, r] * x[r - 1]
+        total = total + t[2, r] * pltpu.roll(here, n - 1, 0) + t[3, r] * pltpu.roll(here, 1, 0)
+        return total + t[4, r] * pltpu.roll(here, m - 1, 1) + t[5, r] * pltpu.roll(here, 1, 1)
+
+    def first(r, carry):
+        here = row_in(r, N0, 4)
+        bc = bo[r + 1] * here
+        be = bo[r + 2] * row_in(r + 1, N0, 4)
+        bw = bo[r] * row_in(r - 1, N0, 4)
+        bn, bs = pltpu.roll(bc, 7, 0), pltpu.roll(bc, 1, 0)
+        bu = jnp.where(lanes3[0:8] == 255, 0.0, pltpu.roll(bc, 255, 1))
+        bd = jnp.where(lanes3[0:8] == 0, 0.0, pltpu.roll(bc, 1, 1))
+        c = [0.5 * (bc + v) for v in (be, bw, bn, bs, bu, bd)]
+        inv = here / (af[0, r] + c[0] + c[1] + c[2] + c[3] + c[4] + c[5])
+        for n in range(4):
+            to[n, r] = c[n] * inv
+        to[4, r] = jnp.where(lanes3[0:8] == 255, 0.0, c[4] * inv)
+        to[5, r] = jnp.where(lanes3[0:8] == 0, 0.0, c[5] * inv)
+        fd = af[1, r] * inv
+        fdo[r] = fd
+        xo[0, r] = fd * (1.0 / smooth_middle)
+        return carry
+
+    def second(r, carry):
+        here = xo[0, r]
+        total = scaled_residual(to, fdo, xo.at[0], r)
+        xo[1, r] = here + smooth_pairs[0][0] * here + smooth_pairs[0][1] * total
+        return carry
+
+    own[2].wait()
+    for copy in along:
+        copy.wait_recv()
+    lax.fori_loop(0, 24, first, 0, unroll=6)
+    lax.fori_loop(1, 23, second, 0, unroll=11)
+    for r in (0, 23):
+        xo[1, r] = jnp.zeros_like(xo[1, r])
+    x12 = []
+    for k, (db, src_at, dst_at) in enumerate(((1, 5, 1), (-1, 2, 6))):
+        x12.append(
+            remote(
+                xo.at[:, :, pl.ds(src_at, 1), :], xr.at[:, :, pl.ds(dst_at, 1), :],
+                s_x12.at[k], r_x12.at[k], device(0, db),
+            )
+        )
+    started += x12
+
     for n in range(2):
         pack(lambda r, n=n: ab4[n, 6 + r, 6:10, :], 4 * n)
     packed = 0.125 * dot(z5[...], gather)
@@ -201,21 +275,23 @@
     x5a[...] = jnp.zeros_like(x5a)
     x5b[...] = jnp.zeros_like(x5b)
 
-    for copy in p1[:16]:
-        copy.wait_recv()
-
-    def inside(start, shape, axis, count):
-        at = lax.broadcasted_iota(jnp.int32, shape, axis) + start
-        return (at >= 0) & (at < count)
-
-    lanes3 = lax.broadcasted_iota(jnp.int32, (16, 256), 1)
+    def place(r, carry):
+        b3[r, 8:16, :] = bo[r]
+        return carry
+
+    def place2(r, carry):
+        a3[r, 4:12, :] = af[0, r]
+        f3[r, 4:12, :] = af[1, r]
+        return carry
+
+    lax.fori_loop(0, 26, place, 0, unroll=13)
+    lax.fori_loop(0, 24, place2, 0, unroll=8)
+    for copy in p1[:12]:
+        copy.wait_recv()
+
     m3c = inside(N1 * b - 4, (16, 256), 0, N1 * NB)
     m3n = inside(N1 * b - 3, (16, 256), 0, N1 * NB)
     m3s = inside(N1 * b - 5, (16, 256), 0, N1 * NB)
-
-    def row_in(r, size, origin):
-        at = size * g + r - origin
-        return jnp.where((at >= 0) & (at < size * NG), 1.0, 0.0).astype(F32)
 
     def table3(r, carry):
         here = row_in(r, N0, 4)
@@ -244,20 +320,24 @@
         x3a[r] = jnp.zeros_like(fd)
         return carry
 
-    smooth_middle, smooth_pairs = coefficients(SMOOTH, SMOOTH_LOW)
     lax.fori_loop(0, 24, table3, 0, unroll=4)
-    own[2].wait()
-    for copy in p1[16:]:
+    for copy in p1[12:]:
         copy.wait_recv()
     lax.fori_loop(0, 24, start3, 0, unroll=8)
-
-    def scaled_residual(t, fd, x, r):
-        here = x[r]
-        n, m = here.shape
-        total = fd[r] - here
-        total = total + t[0, r] * x[r + 1] + t[1, r] * x[r - 1]
-        total = total + t[2, r] * pltpu.roll(here, n - 1, 0) + t[3, r] * pltpu.roll(here, 1, 0)
-        return total + t[4, r] * pltpu.roll(here, m - 1, 1) + t[5, r] * pltpu.roll(here, 1, 1)
+    below = jnp.where(b > 0, 1.0, 0.0).astype(F32)
+    above = jnp.where(b < NB - 1, 1.0, 0.0).astype(F32)
+
+    def given(ref, n):
+        def rows(r, carry):
+            ref[r, 1:2, :] = xr[n, r, 1:2, :] * below
+            ref[r, 14:15, :] = xr[n, r, 6:7, :] * above
+            return carry
+
+        lax.fori_loop(0, 24, rows, 0, unroll=8)
+
+    for copy in x12:
+        copy.wait_recv()
+    given(x3b, 0)
 
     def sweep(t, fd, now, old, lo, hi, chunk, pair):
         def rows(k, carry):
@@ -274,6 +354,7 @@
         lax.fori_loop(0, (hi - lo) // chunk, rows, 0)
 
     sweep(t3, fd3, x3b, x3a, 1, 23, 11, smooth_pairs[0])
+    given(x3a, 1)
     sweep(t3, fd3, x3a, x3b, 2, 22, 10, smooth_pairs[1])
     sweep(t3, fd3, x3b, x3a, 3, 21, 9, smooth_pairs[2])
 
@@ -301,6 +382,21 @@
             halo(inner(h3, 4, 4), window(h3), 0, db, 4, 4, 4, 4, (N0, N1), s_x3.at[k], r_x3.at[k])
         )
     started += x3_copies
+    late = []
+    for k, (db, b_at, b_to, a_at, a_to) in enumerate(((1, 4, 4, 5, 1), (-1, 3, 3, 2, 6))):
+        late.append(
+            remote(
+                bo.at[:, pl.ds(b_at, 1), :], lb.at[:, pl.ds(b_to, 1), :],
+                s_late.at[0, k], r_late.at[0, k], device(0, db),
+            )
+        )
+        late.append(
+            remote(
+                af.at[:, :, pl.ds(a_at, 1), :], lz.at[:, :, pl.ds(a_to, 1), :],
+                s_late.at[1, k], r_late.at[1, k], device(0, db),
+            )
+        )
+    started += late
 
     for copy in abb:
         copy.wait_recv()
@@ -453,6 +549,30 @@
         return carry
 
     lax.fori_loop(1, SPAN - 1, table5, 0)
+
+    for copy in late:
+        copy.wait_recv()
+
+    def widen(r, carry):
+        b3[r, 4:5, :] = lb[r, 4:5, :]
+        b3[r, 19:20, :] = lb[r, 3:4, :]
+        return carry
+
+    def widen2(r, carry):
+        a3[r, 1:2, :] = lz[0, r, 1:2, :]
+        a3[r, 14:15, :] = lz[0, r, 6:7, :]
+        f3[r, 1:2, :] = lz[1, r, 1:2, :]
+        f3[r, 14:15, :] = lz[1, r, 6:7, :]
+        return carry
+
+    def restart3(r, carry):
+        fd3[r] = f3[r] * fd3[r]
+        return carry
+
+    lax.fori_loop(0, 26, widen, 0, unroll=13)
+    lax.fori_loop(0, 24, widen2, 0, unroll=8)
+    lax.fori_loop(0, 24, table3, 0, unroll=4)
+    lax.fori_loop(0, 24, restart3, 0, unroll=8)
     for copy in started:
         copy.wait_send()
     started = []
@@ -571,6 +691,8 @@
 
 SCRATCH = (
     [pltpu.VMEM(shape, F32) for shape in (
+        (26, 8, 256), (2, 24, 8, 256), (6, 24, 8, 256), (24, 8, 256), (2, 24, 8, 256), (2, 24, 8, 256),
+        (26, 8, 256), (2, 24, 8, 256),
         (24, 16, 256), (24, 16, 256), (26, 24, 256), (6, 24, 16, 256), (24, 16, 256), (24, 16, 256),
         (24, 16, 256), (24, 16, 256), (24, 16, 256),
         (2, 20, 16, 128), (20, 16, 128), (2, 20, 16, 128), (6, 20, 16, 128), (20, 16, 128), (20, 16, 128),
@@ -581,7 +703,7 @@
     )]
     + [pltpu.SemaphoreType.DMA((3,)), pltpu.SemaphoreType.REGULAR((2,)), pltpu.SMEM((16, 2), F32)]
     + [pltpu.SemaphoreType.DMA(shape) for count in (
-        (3, 8), (6,), (8,), (4,), (6,), (3,), (2 * MID,), (1,), (3,), (2 * REACH,), (3,)
+        (3, 8), (2,), (2, 2), (6,), (8,), (4,), (6,), (3,), (2 * MID,), (1,), (3,), (2 * REACH,), (3,)
     ) for shape in (count, count)]
 )
 

time: 50.9 us -> 49.6 us (0.974)
  Pallas kernels: 49.2 us -> 48 us
    pallas_call x1, Pallas kernels: 49.2 us -> 48 us  [cycle(): pl.pallas_call(kernel, out_shape=jax.ShapeDtypeStruct((N0, N1, N2), F32),...]
where the time goes in v4:
time: 49.6 us
  Pallas kernels  48 us (97%)
  local copies, waits for them, and re-layouts  1.57 us (3%)
    pallas_call x1, Pallas kernels, cycle(): pl.pallas_call(kernel, out_shape=jax.ShapeDtypeStruct((N0, N1, N2), F32),...  48 us
    unnamed x1, local copies, waits for them, and re-layouts  1.57 us

profile of v4, /device:TPU:1, one launch (start us, length us, event | category | flops | bytes accessed | tf_op | source)
XLA Modules:
  0.0 49.6 jit_solution(2600640787956949297)
XLA Ops:
  0.0 48.0 %vcycle.1 = f32[16,8,256]{2,1,0:T(8,128)} custom-call(f32[16,8,256]{2,1,0:T(8,128)} %source.1, f32[16,8,256]{2,1,0:T(8,128)} %alpha.1, f32[16,8,256]{2,1,0:T(8,128)} %beta.1), custom_call_target="tpu_custom_call" | custom-call | tf_op jit(solution)/shard_map/vcycle/pallas_call | solution.py:712
  48.0 1.6 %copy.5 = f32[16,8,256]{2,1,0:T(8,128)} copy(f32[16,8,256]{2,1,0:T(8,128)} %vcycle.1) | data formatting | bytes 262144

commit v5 on v4

--- a/solution.py
+++ b/solution.py
@@ -81,13 +81,12 @@
     for copy in own:
         copy.start()
 
-    f4[...] = jnp.zeros_like(f4)
-
     partners = FACES + [(0, -8), (0, 8)]
     barrier = pltpu.get_barrier_semaphore()
     for dg, db in partners:
         pl.semaphore_signal(barrier, inc=1, device_id=device(dg, db), device_id_type=MESH)
 
+    f4[...] = jnp.zeros_like(f4)
     pl.semaphore_wait(barrier, len(partners))
 
     def halo(src, dst, dg, db, w0, w1, o0, o1, size, send, recv):
@@ -681,12 +680,19 @@
     sweep(t3, fd3, x3b, x3a, 1, 23, 11, (1.0 / smooth_middle,))
     sweep(t3, fd3, x3a, x3b, 2, 22, 10, smooth_pairs[0])
     sweep(t3, fd3, x3b, x3a, 3, 21, 9, smooth_pairs[1])
-    sweep(t3, fd3, x3a, x3b, 4, 20, 8, smooth_pairs[2])
-    result = pltpu.make_async_copy(x3b.at[pl.ds(4, N0), pl.ds(4, N1), :], out, own_sem.at[0])
-    result.start()
     for copy in started:
         copy.wait_send()
-    result.wait()
+
+    def last(k, carry):
+        for i in range(8):
+            r = 4 + 8 * k + i
+            total = scaled_residual(t3, fd3, x3a, r)
+            here = x3a[r]
+            line = here + smooth_pairs[2][0] * (here - x3b[r]) + smooth_pairs[2][1] * total
+            out[r - 4] = line[4:12]
+        return carry
+
+    lax.fori_loop(0, 2, last, 0)
 
 
 SCRATCH = (
@@ -711,9 +717,9 @@
 def cycle(source, alpha, beta):
     return pl.pallas_call(
         kernel,
-        out_shape=jax.ShapeDtypeStruct((N0, N1, N2), F32),
+        out_shape=pltpu.VMEM((N0, N1, N2), F32),
         in_specs=[pl.BlockSpec(memory_space=pl.ANY)] * 3,
-        out_specs=pl.BlockSpec(memory_space=pl.ANY),
+        out_specs=pl.BlockSpec(memory_space=pltpu.VMEM),
         scratch_shapes=SCRATCH,
         compiler_params=pltpu.CompilerParams(
             collective_id=0, has_side_effects=True, vmem_limit_bytes=63 << 20

time: 49.6 us -> 48.1 us (0.970)
  local copies, waits for them, and re-layouts: 1.57 us -> 0.66 us
  Pallas kernels: 48 us -> 47.3 us
    unnamed x1, local copies, waits for them, and re-layouts: 1.57 us -> 0.66 us
    pallas_call x1, Pallas kernels: 48 us -> 47.3 us  [cycle(): pl.pallas_call(kernel, out_shape=pltpu.VMEM((N0, N1, N2), F32), in_specs=...]
where the time goes in v5:
time: 48.1 us; the launch traced here: 48 us
  Pallas kernels  47.3 us (98%)
  local copies, waits for them, and re-layouts  0.66 us (1%)
    pallas_call x1, Pallas kernels, cycle(): pl.pallas_call(kernel, out_shape=pltpu.VMEM((N0, N1, N2), F32), in_specs=...  47.3 us

profile of v5, /device:TPU:1, one launch (start us, length us, event | category | flops | bytes accessed | tf_op | source)
XLA Modules:
  0.0 48.0 jit_solution(12454511068626327446)
XLA Ops:
  0.0 47.3 %vcycle.1 = f32[16,8,256]{2,1,0:T(8,128)S(1)} custom-call(f32[16,8,256]{2,1,0:T(8,128)} %source.1, f32[16,8,256]{2,1,0:T(8,128)} %alpha.1, f32[16,8,256]{2,1,0:T(8,128)} %beta.1), custom_call_target="tpu_custom_call" | custom-call | tf_op jit(solution)/shard_map/vcycle/pallas_call | solution.py:718
  47.3 0.7 %copy.5 = f32[16,8,256]{2,1,0:T(8,128)} copy(f32[16,8,256]{2,1,0:T(8,128)S(1)} %vcycle.1) | data formatting | bytes 262144

commit v6 on v5

--- a/solution.py
+++ b/solution.py
@@ -229,6 +229,28 @@
         )
     started += x12
 
+    def boxes4(ref, send, recv):
+        copies = []
+        for k, db in enumerate((-2, 2, -1, 1)):
+            copies.append(
+                halo(inner2(ref, 6, 6), window2(ref), 0, db, 6, 6, 6, 6, (8, 4), send.at[k], recv.at[k])
+            )
+        return copies
+
+    def groups4(ref, send, recv):
+        copies = []
+        for k, dg in enumerate((-1, 1)):
+            s0, t0, l0 = part(dg, 8, 6, 6)
+            copies.append(
+                remote(
+                    ref.at[:, pl.ds(6 + s0, l0)], ref.at[:, pl.ds(t0, l0)],
+                    send.at[4 + k], recv.at[4 + k], device(dg, 0),
+                )
+            )
+        return copies
+
+    ab4_boxes = boxes4(ab4, s_ab4, r_ab4)
+    started += ab4_boxes
     for n in range(2):
         pack(lambda r, n=n: ab4[n, 6 + r, 6:10, :], 4 * n)
     packed = 0.125 * dot(z5[...], gather)
@@ -247,28 +269,6 @@
         )
     started += abb
 
-    def boxes4(ref, send, recv):
-        copies = []
-        for k, db in enumerate((-2, 2, -1, 1)):
-            copies.append(
-                halo(inner2(ref, 6, 6), window2(ref), 0, db, 6, 6, 6, 6, (8, 4), send.at[k], recv.at[k])
-            )
-        return copies
-
-    def groups4(ref, send, recv):
-        copies = []
-        for k, dg in enumerate((-1, 1)):
-            s0, t0, l0 = part(dg, 8, 6, 6)
-            copies.append(
-                remote(
-                    ref.at[:, pl.ds(6 + s0, l0)], ref.at[:, pl.ds(t0, l0)],
-                    send.at[4 + k], recv.at[4 + k], device(dg, 0),
-                )
-            )
-        return copies
-
-    ab4_boxes = boxes4(ab4, s_ab4, r_ab4)
-    started += ab4_boxes
 
     x4a[...] = jnp.zeros_like(x4a)
     x5a[...] = jnp.zeros_like(x5a)
@@ -400,7 +400,7 @@
     for copy in abb:
         copy.wait_recv()
     aba = []
-    for k, dg in enumerate((2, 4, 6)):
+    for k, dg in enumerate((2, -2)):
         aba.append(
             remote(
                 g5ab.at[:, :, :, pl.ds(sub, 1), :], g5ab.at[:, :, :, pl.ds(sub, 1), :],
@@ -465,12 +465,13 @@
         )
     started += fa
 
-    for copy in aba:
-        copy.wait_recv()
-    abc = remote(
-        g5ab.at[:, :, :, mine, :], g5ab.at[:, :, :, mine, :], s_abc.at[0], r_abc.at[0], partner
-    )
-    started.append(abc)
+    forward = []
+    for k, (dg, first, size) in enumerate(((2, 0, MID + 1), (-2, MID + 1, MID))):
+        aba[k].wait_recv()
+        other = 4 * core + lax.rem(chip + (3, 1)[k], 4)
+        block = g5ab.at[:, pl.ds(first, size), :, pl.ds(other, 1), :]
+        forward.append(remote(block, block, s_aba.at[2 + k], r_aba.at[2 + k], device(dg, 0)))
+    started += forward
 
     for copy in x3_copies:
         copy.wait_recv()
@@ -501,6 +502,13 @@
     started += fb
     p4_boxes = boxes4(p4, s_p4, r_p4)
     started += p4_boxes
+
+    for copy in forward:
+        copy.wait_recv()
+    abc = remote(
+        g5ab.at[:, :, :, mine, :], g5ab.at[:, :, :, mine, :], s_abc.at[0], r_abc.at[0], partner
+    )
+    started.append(abc)
 
     abc.wait_recv()
     lanes5 = lax.broadcasted_iota(jnp.int32, (8, 128), 1)
@@ -709,7 +717,7 @@
     )]
     + [pltpu.SemaphoreType.DMA((3,)), pltpu.SemaphoreType.REGULAR((2,)), pltpu.SMEM((16, 2), F32)]
     + [pltpu.SemaphoreType.DMA(shape) for count in (
-        (3, 8), (2,), (2, 2), (6,), (8,), (4,), (6,), (3,), (2 * MID,), (1,), (3,), (2 * REACH,), (3,)
+        (3, 8), (2,), (2, 2), (6,), (8,), (4,), (6,), (4,), (2 * MID,), (1,), (3,), (2 * REACH,), (3,)
     ) for shape in (count, count)]
 )
 

time: 48.1 us -> 46 us (0.956)
  Pallas kernels: 47.3 us -> 45.3 us
    pallas_call x1, Pallas kernels: 47.3 us -> 45.3 us  [cycle(): pl.pallas_call(kernel, out_shape=pltpu.VMEM((N0, N1, N2), F32), in_specs=...]
where the time goes in v6:
time: 46 us; the launch traced here: 45.9 us
  Pallas kernels  45.3 us (98%)
  local copies, waits for them, and re-layouts  0.66 us (1%)
    pallas_call x1, Pallas kernels, cycle(): pl.pallas_call(kernel, out_shape=pltpu.VMEM((N0, N1, N2), F32), in_specs=...  45.3 us

profile of v6, /device:TPU:1, one launch (start us, length us, event | category | flops | bytes accessed | tf_op | source)
XLA Modules:
  0.0 45.9 jit_solution(18015869330987239235)
XLA Ops:
  0.0 45.3 %vcycle.1 = f32[16,8,256]{2,1,0:T(8,128)S(1)} custom-call(f32[16,8,256]{2,1,0:T(8,128)} %source.1, f32[16,8,256]{2,1,0:T(8,128)} %alpha.1, f32[16,8,256]{2,1,0:T(8,128)} %beta.1), custom_call_target="tpu_custom_call" | custom-call | tf_op jit(solution)/shard_map/vcycle/pallas_call | solution.py:726
  45.3 0.7 %copy.5 = f32[16,8,256]{2,1,0:T(8,128)} copy(f32[16,8,256]{2,1,0:T(8,128)S(1)} %vcycle.1) | data formatting | bytes 262144

commit v7 on v6

--- a/solution.py
+++ b/solution.py
@@ -52,7 +52,7 @@
     source, alpha, beta, out,
     bo, af, to, fdo, xo, xr, lb, lz, f3, a3, b3, t3, d3, fd3, x3a, x3b, h3,
     ab4, f4, p4, t4, inv4, d4, fd4, x4a, x4b, w4,
-    z5, g5ab, g5f, t5, inv5, fd5, x5a, x5b, q4, w3, u4,
+    z5, g5ab, g5f, m5, c5, t5, inv5, fd5, x5a, x5b, q4, w3, u4,
     own_sem, hello, ends,
     s_p1, r_p1, s_x12, r_x12, s_late, r_late, s_ab4, r_ab4, s_f4, r_f4, s_x3, r_x3, s_p4, r_p4,
     s_aba, r_aba, s_abb, r_abb, s_abc, r_abc, s_fa, r_fa, s_fb, r_fb, s_fc, r_fc,
@@ -455,6 +455,7 @@
     packed = 0.125 * dot(z5[...], gather)
     for i in range(4):
         g5f[MID, i, pl.ds(sub, 1), :] = packed[i : i + 1]
+    early = len(started)
     fa = []
     for k, dg in enumerate((2, 4, 6)):
         fa.append(
@@ -510,6 +511,33 @@
     )
     started.append(abc)
 
+    for copy in late:
+        copy.wait_recv()
+
+    def widen(r, carry):
+        b3[r, 4:5, :] = lb[r, 4:5, :]
+        b3[r, 19:20, :] = lb[r, 3:4, :]
+        return carry
+
+    def widen2(r, carry):
+        a3[r, 1:2, :] = lz[0, r, 1:2, :]
+        a3[r, 14:15, :] = lz[0, r, 6:7, :]
+        f3[r, 1:2, :] = lz[1, r, 1:2, :]
+        f3[r, 14:15, :] = lz[1, r, 6:7, :]
+        return carry
+
+    def restart3(r, carry):
+        fd3[r] = f3[r] * fd3[r]
+        return carry
+
+    lax.fori_loop(0, 26, widen, 0, unroll=13)
+    lax.fori_loop(0, 24, widen2, 0, unroll=8)
+    lax.fori_loop(0, 24, table3, 0, unroll=4)
+    lax.fori_loop(0, 24, restart3, 0, unroll=8)
+    for copy in started[:early]:
+        copy.wait_send()
+    started = started[early:]
+
     abc.wait_recv()
     lanes5 = lax.broadcasted_iota(jnp.int32, (8, 128), 1)
     subs5 = lax.broadcasted_iota(jnp.int32, (8, 128), 0)
@@ -528,61 +556,51 @@
         at = b + k - MID
         return jnp.where((at >= 0) & (at < NB), 1.0, 0.0).astype(F32)
 
-    def beta5(k, i):
-        return g5ab[1, k, i] * box_in(k)
-
-    def table5(k, carry):
-        bc = [beta5(k, i) for i in range(4)]
-        half = [pltpu.roll(v, 64, 1) for v in bc]
-        after = [pltpu.roll(beta5(k + 1, i), 64, 1) for i in range(4)]
-        before = [pltpu.roll(beta5(k - 1, i), 64, 1) for i in range(4)]
+    def fold_even(get, t, i):
+        return pltpu.roll(jnp.where(low, get(2 * MID - t, i), get(t, i)), 64, 1)
+
+    def fold_odd(get, t, i):
+        return jnp.where(low, get(t + 1, i), get(2 * MID - 1 - t, i))
+
+    def fold5(t, carry):
+        here = (2 * t, 2 * t + 1)
+        m5[here[0]] = jnp.where(low, box_in(t), box_in(2 * MID - t))
+        m5[here[1]] = jnp.where(low, box_in(t + 1), box_in(2 * MID - 1 - t))
+        for i in range(4):
+            for n in range(2):
+                def get(k, i, n=n):
+                    return g5ab[n, k, i]
+
+                for a, fold in zip(here, (fold_even, fold_odd)):
+                    value = fold(get, t, i)
+                    c5[n, a, i] = value * m5[a] if n else value
+        return carry
+
+    lax.fori_loop(0, MID, fold5, 0)
+    for i in range(4):
+        c5[1, 2 * MID, i] = pltpu.roll(c5[1, 2 * MID - 1, i], 64, 1)
+
+    def table5(a, carry):
+        bc = [c5[1, a, i] for i in range(4)]
+        mask = m5[a]
         for i in range(4):
             be = bc[i + 1] if i < 3 else jnp.where(subs5 == 7, 0.0, next_group(bc[0]))
             bw = bc[i - 1] if i > 0 else jnp.where(subs5 == 0, 0.0, last_group(bc[3]))
-            bn = jnp.where(low, half[i], after[i])
-            bs = jnp.where(low, before[i], half[i])
             bu = jnp.where(up_end, 0.0, pltpu.roll(bc[i], 127, 1))
             bd = jnp.where(down_end, 0.0, pltpu.roll(bc[i], 1, 1))
-            c = [0.03125 * (bc[i] + v) for v in (be, bw, bn, bs, bu, bd)]
-            diag = g5ab[0, k, i] + c[0] + c[1] + c[2] + c[3] + c[4] + c[5]
-            inv = box_in(k) / diag
-            t5[0, k, i] = c[0] * inv if i < 3 else jnp.where(subs5 == 7, 0.0, c[0] * inv)
-            t5[1, k, i] = c[1] * inv if i > 0 else jnp.where(subs5 == 0, 0.0, c[1] * inv)
-            t5[2, k, i] = c[2] * inv
-            t5[3, k, i] = c[3] * inv
-            t5[4, k, i] = jnp.where(up_end, 0.0, c[4] * inv)
-            t5[5, k, i] = jnp.where(down_end, 0.0, c[5] * inv)
-            inv5[k, i] = inv
-        return carry
-
-    lax.fori_loop(1, SPAN - 1, table5, 0)
-
-    for copy in late:
-        copy.wait_recv()
-
-    def widen(r, carry):
-        b3[r, 4:5, :] = lb[r, 4:5, :]
-        b3[r, 19:20, :] = lb[r, 3:4, :]
-        return carry
-
-    def widen2(r, carry):
-        a3[r, 1:2, :] = lz[0, r, 1:2, :]
-        a3[r, 14:15, :] = lz[0, r, 6:7, :]
-        f3[r, 1:2, :] = lz[1, r, 1:2, :]
-        f3[r, 14:15, :] = lz[1, r, 6:7, :]
-        return carry
-
-    def restart3(r, carry):
-        fd3[r] = f3[r] * fd3[r]
-        return carry
-
-    lax.fori_loop(0, 26, widen, 0, unroll=13)
-    lax.fori_loop(0, 24, widen2, 0, unroll=8)
-    lax.fori_loop(0, 24, table3, 0, unroll=4)
-    lax.fori_loop(0, 24, restart3, 0, unroll=8)
-    for copy in started:
-        copy.wait_send()
-    started = []
+            c = [0.03125 * (bc[i] + v) for v in (be, bw, c5[1, a + 1, i], c5[1, a - 1, i], bu, bd)]
+            inv = mask / (c5[0, a, i] + c[0] + c[1] + c[2] + c[3] + c[4] + c[5])
+            t5[0, a, i] = c[0] * inv if i < 3 else jnp.where(subs5 == 7, 0.0, c[0] * inv)
+            t5[1, a, i] = c[1] * inv if i > 0 else jnp.where(subs5 == 0, 0.0, c[1] * inv)
+            t5[2, a, i] = c[2] * inv
+            t5[3, a, i] = c[3] * inv
+            t5[4, a, i] = jnp.where(up_end, 0.0, c[4] * inv)
+            t5[5, a, i] = jnp.where(down_end, 0.0, c[5] * inv)
+            inv5[a, i] = inv
+        return carry
+
+    lax.fori_loop(1, 2 * MID, table5, 0)
+
 
     fc = []
     for k, (first, last) in enumerate(((MID - 3, MID + 3), (1, MID - 4), (MID + 4, SPAN - 2))):
@@ -605,64 +623,54 @@
         ends[m, 1] = F32(c2)
     for copy in fc:
         copy.wait_recv()
-    for k in range(1, SPAN - 1):
+    for a in range(1, 2 * MID):
         for i in range(4):
-            fd = g5f[k, i] * inv5[k, i]
-            fd5[k, i] = fd
-            x5b[k, i] = fd * (1.0 / bottom_middle)
-
-    def sweep5(now, old, reach, c1, c2):
-        lo, hi = MID - reach, MID + reach + 1
-        half = {}
-
-        def turned(k, i):
-            if (k, i) not in half:
-                half[k, i] = pltpu.roll(now[k, i], 64, 1)
-            return half[k, i]
-
-        for k in range(lo, hi):
-            x = [now[k, i] for i in range(4)]
+            folded = (fold_odd if a % 2 else fold_even)(lambda k, i: g5f[k, i], a // 2, i)
+            fd = folded * inv5[a, i]
+            fd5[a, i] = fd
+            x5b[a, i] = fd * (1.0 / bottom_middle)
+
+    def sweep5(now, old, first, c1, c2):
+        for a in range(first, 2 * MID):
+            x = [now[a, i] for i in range(4)]
             for i in range(4):
                 east = x[i + 1] if i < 3 else next_group(x[0])
                 west = x[i - 1] if i > 0 else last_group(x[3])
-                north = jnp.where(low, turned(k, i), turned(k + 1, i))
-                south = jnp.where(low, turned(k - 1, i), turned(k, i))
-                total = fd5[k, i] - x[i]
-                total = total + t5[0, k, i] * east + t5[1, k, i] * west
-                total = total + t5[2, k, i] * north + t5[3, k, i] * south
-                total = total + t5[4, k, i] * pltpu.roll(x[i], 127, 1) + t5[5, k, i] * pltpu.roll(x[i], 1, 1)
-                old[k, i] = x[i] + c1 * (x[i] - old[k, i]) + c2 * total
-
-    def two(reach, first):
+                inward = now[a + 1, i] if a < 2 * MID - 1 else pltpu.roll(x[i], 64, 1)
+                total = fd5[a, i] - x[i]
+                total = total + t5[0, a, i] * east + t5[1, a, i] * west
+                total = total + t5[2, a, i] * inward + t5[3, a, i] * now[a - 1, i]
+                total = total + t5[4, a, i] * pltpu.roll(x[i], 127, 1) + t5[5, a, i] * pltpu.roll(x[i], 1, 1)
+                old[a, i] = x[i] + c1 * (x[i] - old[a, i]) + c2 * total
+
+    def two(first):
         def body(k, carry):
             m = first + 2 * k
-            sweep5(x5b, x5a, reach, ends[m, 0], ends[m, 1])
-            sweep5(x5a, x5b, reach - 1, ends[m + 1, 0], ends[m + 1, 1])
+            sweep5(x5b, x5a, first + 2, ends[m, 0], ends[m, 1])
+            sweep5(x5a, x5b, first + 3, ends[m + 1, 0], ends[m + 1, 1])
             return carry
 
         return body
 
-    lax.fori_loop(0, 2, two(9, 0), 0)
-    lax.fori_loop(0, 2, two(7, 4), 0)
-    lax.fori_loop(0, 2, two(5, 8), 0)
-    two(3, 12)(0, 0)
-    sweep5(x5b, x5a, 2, ends[14, 0], ends[14, 1])
+    for first in range(0, 14, 2):
+        two(first)(0, 0)
+    sweep5(x5b, x5a, 16, ends[14, 0], ends[14, 1])
 
     for a in range(10):
         row = a - 3
         group = lax.rem(g + (row // 4) + NG, NG)
         at = 4 * lax.rem(group, 2) + group // 2
-        for k in range(5):
-            line = x5a[MID - 2 + k, row % 4, pl.ds(at, 1), :]
-            first, last = max(4 * k - 2, 0), min(4 * k + 2, 16)
-            q4[a, first:last, :] = jnp.broadcast_to(line, (last - first, 128))
+        for k in range(4):
+            line = jnp.broadcast_to(x5a[16 + k, row % 4, pl.ds(at, 1), :], (2, 128))
+            q4[a, 2 * k : 2 * k + 2, :] = line
+            q4[a, 14 - 2 * k : 16 - 2 * k, :] = line
     grown = dot(q4[...].reshape(160, 128), spread).reshape(10, 16, 256)
     rows4 = lax.broadcasted_iota(jnp.int32, (16, 128), 0)
-    first_of_box = lax.rem(lax.shift_right_logical(rows4 + 2, 1), 2) == 0
+    first_half = rows4 < 8
     for copy in p4_groups:
         copy.wait_recv()
     for a in range(10):
-        line = jnp.where(first_of_box, grown[a, :, 0:128], grown[a, :, 128:256])
+        line = jnp.where(first_half, grown[a, :, 0:128], grown[a, :, 128:256])
         for r in (2 * a, 2 * a + 1):
             x4b[r] = jnp.where(m4, p4[1, r] + line, 0.0) * row_in(r, 8, 6)
             if 1 <= r < 19:
@@ -711,7 +719,8 @@
         (24, 16, 256), (24, 16, 256), (24, 16, 256),
         (2, 20, 16, 128), (20, 16, 128), (2, 20, 16, 128), (6, 20, 16, 128), (20, 16, 128), (20, 16, 128),
         (20, 16, 128), (20, 16, 128), (20, 16, 128), (8, 16, 128),
-        (8, 256), (2, SPAN, 4, 8, 128), (SPAN, 4, 8, 128), (6, SPAN, 4, 8, 128), (SPAN, 4, 8, 128),
+        (8, 256), (2, SPAN, 4, 8, 128), (SPAN, 4, 8, 128),
+        (SPAN, 8, 128), (2, SPAN, 4, 8, 128), (6, SPAN, 4, 8, 128), (SPAN, 4, 8, 128),
         (SPAN, 4, 8, 128), (SPAN, 4, 8, 128), (SPAN, 4, 8, 128), (10, 16, 128), (8, 16, 256),
         (2, 12, 16, 128),
     )]

time: 46 us -> 45.4 us (0.987)
  Pallas kernels: 45.3 us -> 44.6 us
    pallas_call x1, Pallas kernels: 45.3 us -> 44.6 us  [cycle(): pl.pallas_call(kernel, out_shape=pltpu.VMEM((N0, N1, N2), F32), in_specs=...]
where the time goes in v7:
time: 45.4 us; the launch traced here: 45.3 us
  Pallas kernels  44.6 us (98%)
  local copies, waits for them, and re-layouts  0.66 us (1%)
    pallas_call x1, Pallas kernels, cycle(): pl.pallas_call(kernel, out_shape=pltpu.VMEM((N0, N1, N2), F32), in_specs=...  44.6 us

profile of v7, /device:TPU:1, one launch (start us, length us, event | category | flops | bytes accessed | tf_op | source)
XLA Modules:
  0.0 45.3 jit_solution(17314136781784036443)
XLA Ops:
  0.0 44.6 %vcycle.1 = f32[16,8,256]{2,1,0:T(8,128)S(1)} custom-call(f32[16,8,256]{2,1,0:T(8,128)} %source.1, f32[16,8,256]{2,1,0:T(8,128)} %alpha.1, f32[16,8,256]{2,1,0:T(8,128)} %beta.1), custom_call_target="tpu_custom_call" | custom-call | tf_op jit(solution)/shard_map/vcycle/pallas_call | solution.py:735
  44.6 0.7 %copy.5 = f32[16,8,256]{2,1,0:T(8,128)} copy(f32[16,8,256]{2,1,0:T(8,128)S(1)} %vcycle.1) | data formatting | bytes 262144

commit v8 on v7

--- a/solution.py
+++ b/solution.py
@@ -60,6 +60,9 @@
     g, b = lax.axis_index("grp"), lax.axis_index("box")
     core, chip = lax.rem(g, 2), g // 2
     sub = 4 * core + chip
+
+    mine = pl.ds(pl.multiple_of(4 * core, 4), 4)
+    partner = (g + 1 - 2 * core, b)
 
     def device(dg, db):
         return (lax.rem(g + dg + NG, NG), lax.rem(b + db + NB, NB))
@@ -399,6 +402,13 @@
 
     for copy in abb:
         copy.wait_recv()
+    abc = []
+
+    def share(at):
+        block = g5ab.at[:, :, :, pl.ds(at, 1), :]
+        k = len(abc)
+        abc.append(remote(block, block, s_abc.at[k], r_abc.at[k], partner))
+
     aba = []
     for k, dg in enumerate((2, -2)):
         aba.append(
@@ -408,6 +418,7 @@
             )
         )
     started += aba
+    share(sub)
 
     for copy in ab4_groups:
         copy.wait_recv()
@@ -436,8 +447,6 @@
 
     lax.fori_loop(1, 19, table4, 0, unroll=6)
 
-    mine = pl.ds(pl.multiple_of(4 * core, 4), 4)
-    partner = (g + 1 - 2 * core, b)
 
     for copy in f4_copies:
         copy.wait_recv()
@@ -472,6 +481,7 @@
         other = 4 * core + lax.rem(chip + (3, 1)[k], 4)
         block = g5ab.at[:, pl.ds(first, size), :, pl.ds(other, 1), :]
         forward.append(remote(block, block, s_aba.at[2 + k], r_aba.at[2 + k], device(dg, 0)))
+        share(other)
     started += forward
 
     for copy in x3_copies:
@@ -506,10 +516,8 @@
 
     for copy in forward:
         copy.wait_recv()
-    abc = remote(
-        g5ab.at[:, :, :, mine, :], g5ab.at[:, :, :, mine, :], s_abc.at[0], r_abc.at[0], partner
-    )
-    started.append(abc)
+    share(4 * core + lax.rem(chip + 2, 4))
+    started += abc
 
     for copy in late:
         copy.wait_recv()
@@ -538,7 +546,8 @@
         copy.wait_send()
     started = started[early:]
 
-    abc.wait_recv()
+    for copy in abc:
+        copy.wait_recv()
     lanes5 = lax.broadcasted_iota(jnp.int32, (8, 128), 1)
     subs5 = lax.broadcasted_iota(jnp.int32, (8, 128), 0)
     low = lanes5 < 64
@@ -576,7 +585,7 @@
                     c5[n, a, i] = value * m5[a] if n else value
         return carry
 
-    lax.fori_loop(0, MID, fold5, 0)
+    lax.fori_loop(0, MID, fold5, 0, unroll=5)
     for i in range(4):
         c5[1, 2 * MID, i] = pltpu.roll(c5[1, 2 * MID - 1, i], 64, 1)
 
@@ -599,7 +608,7 @@
             inv5[a, i] = inv
         return carry
 
-    lax.fori_loop(1, 2 * MID, table5, 0)
+    lax.fori_loop(1, 2 * MID, table5, 0, unroll=5)
 
 
     fc = []
@@ -726,7 +735,7 @@
     )]
     + [pltpu.SemaphoreType.DMA((3,)), pltpu.SemaphoreType.REGULAR((2,)), pltpu.SMEM((16, 2), F32)]
     + [pltpu.SemaphoreType.DMA(shape) for count in (
-        (3, 8), (2,), (2, 2), (6,), (8,), (4,), (6,), (4,), (2 * MID,), (1,), (3,), (2 * REACH,), (3,)
+        (3, 8), (2,), (2, 2), (6,), (8,), (4,), (6,), (4,), (2 * MID,), (4,), (3,), (2 * REACH,), (3,)
     ) for shape in (count, count)]
 )
 

time: 45.4 us -> 45.4 us (level)
  no operation moved by 1% of the time
where the time goes in v8:
time: 45.4 us
  Pallas kernels  44.7 us (98%)
  local copies, waits for them, and re-layouts  0.66 us (1%)
    pallas_call x1, Pallas kernels, cycle(): pl.pallas_call(kernel, out_shape=pltpu.VMEM((N0, N1, N2), F32), in_specs=...  44.7 us

profile of v8, /device:TPU:1, one launch (start us, length us, event | category | flops | bytes accessed | tf_op | source)
XLA Modules:
  0.0 45.4 jit_solution(12536931541275799827)
XLA Ops:
  0.0 44.7 %vcycle.1 = f32[16,8,256]{2,1,0:T(8,128)S(1)} custom-call(f32[16,8,256]{2,1,0:T(8,128)} %source.1, f32[16,8,256]{2,1,0:T(8,128)} %alpha.1, f32[16,8,256]{2,1,0:T(8,128)} %beta.1), custom_call_target="tpu_custom_call" | custom-call | tf_op jit(solution)/shard_map/vcycle/pallas_call | solution.py:744
  44.7 0.7 %copy.5 = f32[16,8,256]{2,1,0:T(8,128)} copy(f32[16,8,256]{2,1,0:T(8,128)S(1)} %vcycle.1) | data formatting | bytes 262144

commit v9 on v7

--- a/solution.py
+++ b/solution.py
@@ -376,6 +376,17 @@
         copy.wait_recv()
     ab4_groups = groups4(ab4, s_ab4, r_ab4)
     started += ab4_groups
+    for copy in abb:
+        copy.wait_recv()
+    aba = []
+    for k, dg in enumerate((2, -2)):
+        aba.append(
+            remote(
+                g5ab.at[:, :, :, pl.ds(sub, 1), :], g5ab.at[:, :, :, pl.ds(sub, 1), :],
+                s_aba.at[k], r_aba.at[k], device(dg, 0),
+            )
+        )
+    started += aba
     for k, db in enumerate((-1, 1)):
         x3_copies.append(
             halo(inner(h3, 4, 4), window(h3), 0, db, 4, 4, 4, 4, (N0, N1), s_x3.at[k], r_x3.at[k])
@@ -397,17 +408,6 @@
         )
     started += late
 
-    for copy in abb:
-        copy.wait_recv()
-    aba = []
-    for k, dg in enumerate((2, -2)):
-        aba.append(
-            remote(
-                g5ab.at[:, :, :, pl.ds(sub, 1), :], g5ab.at[:, :, :, pl.ds(sub, 1), :],
-                s_aba.at[k], r_aba.at[k], device(dg, 0),
-            )
-        )
-    started += aba
 
     for copy in ab4_groups:
         copy.wait_recv()

time: 45.4 us -> 45.6 us (level)
  no operation moved by 1% of the time
where the time goes in v9:
time: 45.6 us; the launch traced here: 45.5 us
  Pallas kernels  44.9 us (98%)
  local copies, waits for them, and re-layouts  0.66 us (1%)
    pallas_call x1, Pallas kernels, cycle(): pl.pallas_call(kernel, out_shape=pltpu.VMEM((N0, N1, N2), F32), in_specs=...  44.9 us

profile of v9, /device:TPU:1, one launch (start us, length us, event | category | flops | bytes accessed | tf_op | source)
XLA Modules:
  0.0 45.5 jit_solution(13039543206296775510)
XLA Ops:
  0.0 44.9 %vcycle.1 = f32[16,8,256]{2,1,0:T(8,128)S(1)} custom-call(f32[16,8,256]{2,1,0:T(8,128)} %source.1, f32[16,8,256]{2,1,0:T(8,128)} %alpha.1, f32[16,8,256]{2,1,0:T(8,128)} %beta.1), custom_call_target="tpu_custom_call" | custom-call | tf_op jit(solution)/shard_map/vcycle/pallas_call | solution.py:735
  44.9 0.7 %copy.5 = f32[16,8,256]{2,1,0:T(8,128)} copy(f32[16,8,256]{2,1,0:T(8,128)S(1)} %vcycle.1) | data formatting | bytes 262144
